TPU v7x, 32 devices: a whole 2x2x4 slice. The times are simulated.
32 devices in a mesh: ty: 4 (over y, core), tx: 8 (over z, x).
Axes of the slice: x: 2, y: 2, z: 4, core: 2. Of those that a mesh axis runs over, the one named last changes fastest.
Arguments:
- incident: float32 [2, 1280, 3072], P(None, 'ty', 'tx'), may hold values from -6 to 6
- phases: float32 [2, 1280, 3072], P(None, 'ty', 'tx'), may hold values from -3.140625 to 3.140625
- cotangent: float32 [2, 1280, 3072], P(None, 'ty', 'tx'), may hold values from -6 to 6
- propagator: float32 [2, 33], replicated, may hold values from -0.6 to 0.6
Outputs:
- phase_grad: float32 [2, 1280, 3072], P(None, 'ty', 'tx')
- probe_grad: float32 [2, 1280, 3072], P(None, 'ty', 'tx')
All inputs are finite; a program needn't handle non-finite values.
Results may differ from a plain program's by a relative error of at most 0.00015.
Values sent between devices are 32-bit elements; how exact they have to be, the bound alone decides.
A program may use at most 64 MiB of HBM per device.

v0:
```python
import jax
import jax.numpy as jnp
from jax import lax
from jax.experimental import pallas as pl
from jax.experimental.pallas import tpu as pltpu
from jax.sharding import PartitionSpec as P

RIM = 16
WIDE = 2 * RIM
LANES = 128
OUT = LANES - WIDE
F32 = jnp.float32
BF16 = jnp.bfloat16


def block(rows, most):
    return max(n for n in range(16, most + 1, 16) if rows % n == 0)


def sincos(angle):
    half = angle * 0.5
    sq = half * half
    s = -1.0 / 39916800.0
    for c in (1.0 / 362880.0, -1.0 / 5040.0, 1.0 / 120.0, -1.0 / 6.0):
        s = s * sq + c
    s = half + half * sq * s
    c = 1.0 / 479001600.0
    for k in (-1.0 / 3628800.0, 1.0 / 40320.0, -1.0 / 720.0, 1.0 / 24.0, -0.5, 1.0):
        c = c * sq + k
    return 2.0 * s * c, 1.0 - 2.0 * s * s


def split(x):
    hi = x.astype(BF16)
    return hi, (x - hi.astype(F32)).astype(BF16)


def lanes_of(rows, width=LANES):
    return lax.broadcasted_iota(jnp.int32, (rows, width), 1)


def toeplitz(line, rows, width, shift):
    wide = jnp.broadcast_to(line[:, :width], (rows, width))
    return pltpu.roll(wide, shift % width, 1, stride=1, stride_axis=0)


PIECES = (("c0", WIDE, 0), ("c1", WIDE, 32), ("p1", RIM, 64), ("i0", RIM, 80), ("i1", RIM, 96), ("p0", RIM, 112))


def make_kernel(H, W, tap_shape):
    tiles = W // LANES
    full = W + LANES
    step = block(H, 80)

    def kernel(
        inc, ph, cot, prop, pg, pb,
        incv, phv, cotv, packl, packr, hl, hr, crow, irow, prow,
        taps, line, xh, xl, zh, zl, gh, gl, uh, ul, vh, vl,
        c1, s1, c0, s0, wz, gout, fout, rowf, rowa, colf, cola, colb, pgv, pbv,
        load, store, send, recv,
    ):
        ty, tx = lax.axis_index("ty"), lax.axis_index("tx")
        ny, nx = lax.axis_size("ty"), lax.axis_size("tx")
        up, down = lax.rem(ty + ny - 1, ny), lax.rem(ty + 1, ny)
        left, right = lax.rem(tx + nx - 1, nx), lax.rem(tx + 1, nx)

        loads = [
            pltpu.make_async_copy(src, dst, load.at[k])
            for k, (src, dst) in enumerate(((cot, cotv), (ph, phv), (inc, incv), (prop, taps)))
        ]
        for c in loads:
            c.start()
        barrier = pltpu.get_barrier_semaphore()
        others = [(up, tx), (down, tx), (ty, left), (ty, right), (up, left), (up, right), (down, left), (down, right)]
        for dev in others:
            pl.semaphore_signal(barrier, inc=1, device_id=dev, device_id_type=pl.DeviceIdType.MESH)
        for c in loads:
            c.wait()

        def plane(name):
            return {"c0": (cotv, 0), "c1": (cotv, 1), "p0": (phv, 0), "p1": (phv, 1), "i0": (incv, 0), "i1": (incv, 1)}[name]

        @pl.loop(0, H // step)
        def _(i):
            r = pl.ds(pl.multiple_of(i * step, step), step)
            lane = lanes_of(step)
            a = jnp.zeros((step, LANES), F32)
            b = jnp.zeros((step, LANES), F32)
            for name, w, dst in PIECES:
                ref, p = plane(name)
                first = ref[p, r, 0:LANES]
                last = ref[p, r, W - LANES : W]
                here = (lane >= dst) & (lane < dst + w)
                a = jnp.where(here, pltpu.roll(first, dst, 1) if dst else first, a)
                b = jnp.where(here, pltpu.roll(last, (dst + w) % LANES, 1), b)
            packl[r, :] = a
            packr[r, :] = b

        pl.semaphore_wait(barrier, 8)
        copies = []

        def push(src, dst, dev):
            k = len(copies)
            c = pltpu.make_async_remote_copy(
                src_ref=src, dst_ref=dst, send_sem=send.at[k], recv_sem=recv.at[k],
                device_id=dev, device_id_type=pl.DeviceIdType.MESH,
            )
            c.start()
            copies.append(c)

        push(packl, hr.at[WIDE : WIDE + H], (ty, left))
        push(packr, hl.at[WIDE : WIDE + H], (ty, right))
        push(cot.at[:, 0:WIDE, :], crow.at[1], (up, tx))
        push(cot.at[:, H - WIDE : H, :], crow.at[0], (down, tx))
        push(inc.at[:, 0:RIM, :], irow.at[1], (up, tx))
        push(inc.at[:, H - RIM : H, :], irow.at[0], (down, tx))
        push(ph.at[:, 0:RIM, :], prow.at[1], (up, tx))
        push(ph.at[:, H - RIM : H, :], prow.at[0], (down, tx))
        push(packl.at[0:WIDE], hr.at[WIDE + H : WIDE + H + WIDE], (up, left))
        push(packl.at[H - WIDE : H], hr.at[0:WIDE], (down, left))
        push(packr.at[0:WIDE], hl.at[WIDE + H : WIDE + H + WIDE], (up, right))
        push(packr.at[H - WIDE : H], hl.at[0:WIDE], (down, right))

        line[...] = jnp.zeros(line.shape, F32)
        line[0:2, 0 : prop.shape[1]] = taps[...]
        kr, ki = line[0:1, :], line[1:2, :]

        def rows_band(dst, mr, mi):
            top = jnp.concatenate([mr, -mi], axis=1)
            low = jnp.concatenate([mi, mr], axis=1)
            hi, lo = split(jnp.concatenate([top, low], axis=0))
            k = 2 * LANES
            dst[:, 0:k] = hi
            dst[:, k : 2 * k] = hi
            dst[:, 2 * k : 3 * k] = lo

        def cols_band(dst, tr, ti):
            top = jnp.concatenate([tr, ti], axis=1)
            low = jnp.concatenate([-ti, tr], axis=1)
            hi, lo = split(jnp.concatenate([top, low], axis=0))
            k = 4 * LANES
            dst[0:k, :] = hi
            dst[k : 2 * k, :] = hi
            dst[2 * k : 3 * k, :] = lo

        rows_band(rowf, toeplitz(kr, LANES, LANES, 0)[:OUT], toeplitz(ki, LANES, LANES, 0)[:OUT])
        rows_band(rowa, toeplitz(kr, LANES, LANES, -WIDE).T[:OUT], -toeplitz(ki, LANES, LANES, -WIDE).T[:OUT])
        cols_band(colf, toeplitz(kr, LANES, 2 * LANES, 0).T, toeplitz(ki, LANES, 2 * LANES, 0).T)
        cols_band(
            cola,
            toeplitz(kr, 2 * LANES, 2 * LANES, -WIDE)[:, :LANES],
            -toeplitz(ki, 2 * LANES, 2 * LANES, -WIDE)[:, :LANES],
        )

        cols_band(
            colb,
            toeplitz(kr, 2 * LANES, 2 * LANES, -LANES)[:, :LANES],
            -toeplitz(ki, 2 * LANES, 2 * LANES, -LANES)[:, :LANES],
        )

        def moved(ref, t, r):
            return pltpu.roll(ref[1, r, t * LANES : (t + 1) * LANES], LANES - RIM, 1)

        def phase_one(ref, r, q, rows, which):
            last = lanes_of(rows) >= LANES - RIM
            for t in which:
                s, c = sincos(jnp.where(last, moved(ref, t + 1, r), moved(ref, t, r)))
                s1[q, t * LANES : (t + 1) * LANES] = s
                c1[q, t * LANES : (t + 1) * LANES] = c

        @pl.loop(0, H // 16)
        def _(i):
            r0 = pl.multiple_of(i * 16, 16)
            r = pl.ds(r0, 16)
            for p in range(2):
                hi, lo = split(cotv[p, r, :])
                q = pl.ds(pl.multiple_of(r0 + WIDE, 16), 16)
                xh[p, q, 0:W] = hi
                xl[p, q, 0:W] = lo
            q = pl.ds(pl.multiple_of(r0 + RIM, 16), 16)
            phase_one(phv, r, q, 16, range(tiles - 1))
            s, c = sincos(phv[0, r, :])
            s0[r, :] = s
            c0[r, :] = c
            a, b = incv[0, r, :], incv[1, r, :]
            for p, w in enumerate((a * c - b * s, a * s + b * c)):
                wz[p, r, :] = w
                hi, lo = split(w)
                zh[p, q, 0:W] = hi
                zl[p, q, 0:W] = lo

        for k in (2, 3, 4, 5, 6, 7):
            copies[k].wait_recv()
        for side in range(2):
            q = slice(0, WIDE) if side == 0 else slice(WIDE + H, WIDE + H + WIDE)
            for p in range(2):
                hi, lo = split(crow[side, p])
                xh[p, q, 0:W] = hi
                xl[p, q, 0:W] = lo
            q = slice(0, RIM) if side == 0 else slice(RIM + H, RIM + H + RIM)
            phase_one(prow.at[side], slice(0, RIM), q, RIM, range(tiles - 1))
            s, c = sincos(prow[side, 0])
            a, b = irow[side, 0], irow[side, 1]
            for p, w in enumerate((a * c - b * s, a * s + b * c)):
                hi, lo = split(w)
                zh[p, q, 0:W] = hi
                zl[p, q, 0:W] = lo

        def down_pass(src_h, src_l, dst_h, dst_l, band, rows, lo_lane, hi_lane):
            starts = list(range(0, rows - OUT, OUT)) + [rows - OUT]
            cols = slice(lo_lane, hi_lane)
            for q0 in starts:
                win = slice(q0, q0 + LANES)
                hi = [src_h[0, win, cols], src_h[1, win, cols]]
                lo = [src_l[0, win, cols], src_l[1, win, cols]]
                operand = jnp.concatenate(hi + lo + hi, axis=0)
                u = jnp.dot(band[...], operand, preferred_element_type=F32)
                h, l = split(u)
                for p in range(2):
                    dst_h[p, q0 : q0 + OUT, cols] = h[p * OUT : (p + 1) * OUT]
                    dst_l[p, q0 : q0 + OUT, cols] = l[p * OUT : (p + 1) * OUT]

        def across_pass(src_h, src_l, dst, band, rows, which, first=0):
            for t in which:
                m, n = (t + first) % (tiles + 1), (t + first + 1) % (tiles + 1)
                a, b = slice(m * LANES, (m + 1) * LANES), slice(n * LANES, (n + 1) * LANES)
                hi = [src_h[0, 0:rows, a], src_h[0, 0:rows, b], src_h[1, 0:rows, a], src_h[1, 0:rows, b]]
                lo = [src_l[0, 0:rows, a], src_l[0, 0:rows, b], src_l[1, 0:rows, a], src_l[1, 0:rows, b]]
                operand = jnp.concatenate(hi + lo + hi, axis=1)
                dst[t, 0:rows, :] = jnp.dot(operand, band[...], preferred_element_type=F32)

        down_pass(xh, xl, uh, ul, rowa, H + WIDE, 0, W)
        down_pass(zh, zl, vh, vl, rowf, H, 0, W)
        across_pass(uh, ul, gout, cola, H + WIDE, range(tiles - 1))
        across_pass(vh, vl, fout, colf, H, range(tiles - 1))

        for k in (0, 1, 8, 9, 10, 11):
            copies[k].wait_recv()
        edge = slice(W, full)

        def piece(a, b, index, rows):
            _, w, dst = PIECES[index]
            lane = lanes_of(rows)
            a = pltpu.roll(a, (LANES - w - dst) % LANES, 1)
            b = pltpu.roll(b, (-dst) % LANES, 1) if dst else b
            return jnp.where(lane < w, b, jnp.where(lane >= LANES - w, a, 0.0))

        xstep = block(H + 2 * WIDE, 96)

        @pl.loop(0, (H + 2 * WIDE) // xstep)
        def _(i):
            r = pl.ds(pl.multiple_of(i * xstep, 16), xstep)
            a, b = hl[r, :], hr[r, :]
            for p in range(2):
                hi, lo = split(piece(a, b, p, xstep))
                xh[p, r, edge] = hi
                xl[p, r, edge] = lo

        estep = block(H + WIDE, 64)

        def phase_edge(r, q, own, own_r, rows):
            a, b = hl[q, :], hr[q, :]
            _, _, dst = PIECES[2]
            lane = lanes_of(rows)
            inner = moved(own, tiles - 1, own_r)
            x = jnp.where(lane >= LANES - RIM, pltpu.roll(b, LANES - RIM - dst, 1), inner)
            outer = jnp.where(lane >= LANES - WIDE, pltpu.roll(a, LANES - WIDE - dst, 1), 0.0)
            y = jnp.where(lane >= LANES - RIM, moved(own, 0, own_r), outer)
            for t, v in ((tiles - 1, x), (tiles, y)):
                s, c = sincos(v)
                s1[r, t * LANES : (t + 1) * LANES] = s
                c1[r, t * LANES : (t + 1) * LANES] = c

        hstep = block(H, 64)

        @pl.loop(0, H // hstep)
        def _(i):
            r = pl.ds(pl.multiple_of(i * hstep + RIM, 16), hstep)
            q = pl.ds(pl.multiple_of(i * hstep + WIDE, 16), hstep)
            phase_edge(r, q, phv, pl.ds(pl.multiple_of(i * hstep, 16), hstep), hstep)

        for side in range(2):
            e = side * (H + RIM)
            phase_edge(slice(e, e + RIM), slice(e + RIM, e + WIDE), prow.at[side], slice(0, RIM), RIM)

        @pl.loop(0, (H + WIDE) // estep)
        def _(i):
            r = pl.ds(pl.multiple_of(i * estep, 16), estep)
            q = pl.ds(pl.multiple_of(i * estep + RIM, 16), estep)
            a, b = hl[q, :], hr[q, :]
            s, c = sincos(piece(a, b, 5, estep))
            x, y = piece(a, b, 3, estep), piece(a, b, 4, estep)
            for p, w in enumerate((x * c - y * s, x * s + y * c)):
                hi, lo = split(w)
                zh[p, r, edge] = hi
                zl[p, r, edge] = lo

        down_pass(xh, xl, uh, ul, rowa, H + WIDE, W, full)
        across_pass(uh, ul, gout, cola, H + WIDE, range(tiles - 1, tiles + 1))

        @pl.loop(0, (H + WIDE) // estep)
        def _(i):
            r = pl.ds(pl.multiple_of(i * estep, 16), estep)
            for t in range(tiles + 1):
                cols = slice(t * LANES, (t + 1) * LANES)
                gr, gi = gout[t, r, 0:LANES], gout[t, r, LANES : 2 * LANES]
                c, s = c1[r, cols], s1[r, cols]
                for p, g in enumerate((gr * c + gi * s, gi * c - gr * s)):
                    hi, lo = split(g)
                    gh[p, r, cols] = hi
                    gl[p, r, cols] = lo

        down_pass(zh, zl, vh, vl, rowf, H, W, full)
        across_pass(vh, vl, fout, colf, H, range(tiles - 1, tiles + 1))

        fstep = block(H, 32)

        @pl.loop(0, H // fstep)
        def _(i):
            r = pl.ds(pl.multiple_of(i * fstep, 16), fstep)
            q = pl.ds(pl.multiple_of(i * fstep + RIM, 16), fstep)
            first = lanes_of(fstep) < RIM
            before = None
            for t in [tiles] + list(range(tiles)):
                cols = slice(t * LANES, (t + 1) * LANES)
                gr, gi = gout[t, q, 0:LANES], gout[t, q, LANES : 2 * LANES]
                fr, fi = fout[t, r, 0:LANES], fout[t, r, LANES : 2 * LANES]
                c, s = c1[q, cols], s1[q, cols]
                term = pltpu.roll(gi * (fr * c - fi * s) - gr * (fr * s + fi * c), RIM, 1)
                if before is not None:
                    pgv[1, r, cols] = jnp.where(first, before, term)
                before = term

        stores = [pltpu.make_async_copy(pgv.at[1], pg.at[1], store.at[0])]
        stores[0].start()

        down_pass(gh, gl, vh, vl, rowa, H, 0, full)
        across_pass(vh, vl, fout, colb, H, range(tiles), -1)

        @pl.loop(0, H // fstep)
        def _(i):
            r = pl.ds(pl.multiple_of(i * fstep, 16), fstep)
            for t in range(tiles):
                cols = slice(t * LANES, (t + 1) * LANES)
                gr, gi = fout[t, r, 0:LANES], fout[t, r, LANES : 2 * LANES]
                c, s = c0[r, cols], s0[r, cols]
                pgv[0, r, cols] = gi * wz[0, r, cols] - gr * wz[1, r, cols]
                pbv[0, r, cols] = gr * c + gi * s
                pbv[1, r, cols] = gi * c - gr * s

        stores.append(pltpu.make_async_copy(pgv.at[0], pg.at[0], store.at[1]))
        stores.append(pltpu.make_async_copy(pbv, pb, store.at[2]))
        stores[1].start()
        stores[2].start()
        for c in copies:
            c.wait_send()
        for c in stores:
            c.wait()

    V = pltpu.VMEM
    scratch = [
        V((2, H, W), F32), V((2, H, W), F32), V((2, H, W), F32),
        V((H, LANES), F32), V((H, LANES), F32),
        V((H + 2 * WIDE, LANES), F32), V((H + 2 * WIDE, LANES), F32),
        V((2, 2, WIDE, W), F32), V((2, 2, RIM, W), F32), V((2, 2, RIM, W), F32),
        V(tap_shape, F32), V((8, 2 * LANES), F32),
        V((2, H + 2 * WIDE, full), BF16), V((2, H + 2 * WIDE, full), BF16),
        V((2, H + WIDE, full), BF16), V((2, H + WIDE, full), BF16),
        V((2, H + WIDE, full), BF16), V((2, H + WIDE, full), BF16),
        V((2, H + WIDE, full), BF16), V((2, H + WIDE, full), BF16),
        V((2, H, full), BF16), V((2, H, full), BF16),
        V((H + WIDE, full), F32), V((H + WIDE, full), F32),
        V((H, W), F32), V((H, W), F32), V((2, H, W), F32),
        V((tiles + 1, H + WIDE, 2 * LANES), F32), V((tiles + 1, H, 2 * LANES), F32),
        V((2 * OUT, 6 * LANES), BF16), V((2 * OUT, 6 * LANES), BF16),
        V((12 * LANES, 2 * LANES), BF16), V((12 * LANES, 2 * LANES), BF16),
        V((12 * LANES, 2 * LANES), BF16),
        V((2, H, W), F32), V((2, H, W), F32),
        pltpu.SemaphoreType.DMA((4,)), pltpu.SemaphoreType.DMA((3,)),
        pltpu.SemaphoreType.DMA((12,)), pltpu.SemaphoreType.DMA((12,)),
    ]
    anywhere = pl.BlockSpec(memory_space=pl.ANY)
    return pl.pallas_call(
        kernel,
        out_shape=(jax.ShapeDtypeStruct((2, H, W), F32), jax.ShapeDtypeStruct((2, H, W), F32)),
        in_specs=[pl.BlockSpec(memory_space=pltpu.HBM)] * 4,
        out_specs=(anywhere, anywhere),
        scratch_shapes=scratch,
        compiler_params=pltpu.CompilerParams(
            collective_id=0, has_side_effects=True, vmem_limit_bytes=40 * 1024 * 1024
        ),
        cost_estimate=pl.CostEstimate(flops=10**10, bytes_accessed=5 * 10**6, transcendentals=0),
    )


def on_device(incident, phases, cotangent, propagator):
    H, W = incident.shape[1], incident.shape[2]
    return make_kernel(H, W, propagator.shape)(incident, phases, cotangent, propagator)


def solution(mesh):
    placed = (P(None, "ty", "tx"), P(None, "ty", "tx"), P(None, "ty", "tx"), P())
    return jax.shard_map(
        on_device,
        mesh=mesh,
        in_specs=placed,
        out_specs=(P(None, "ty", "tx"), P(None, "ty", "tx")),
        check_vma=False,
    )
```

profile of v0, /device:TPU:1, one launch (start us, length us, event | category | flops | bytes accessed | tf_op | source)
XLA Modules:
  0.0 32.5 jit_solution(2557241281327161137)
XLA Ops:
  0.6 0.0 copy-start
  0.6 1.2 %copy-done = f32[2,320,384]{2,1,0:T(8,128)S(1)} copy-done((f32[2,320,384]{2,1,0:T(8,128)S(1)}, f32[2,320,384]{2,1,0:T(8,128)}, u32[]{:S(2)}) %copy-start) | copy-done | bytes 983064
  1.8 0.0 copy-start.1
  1.8 1.2 %copy-done.1 = f32[2,320,384]{2,1,0:T(8,128)S(1)} copy-done((f32[2,320,384]{2,1,0:T(8,128)S(1)}, f32[2,320,384]{2,1,0:T(8,128)}, u32[]{:S(2)}) %copy-start.1) | copy-done | bytes 983064
  3.0 0.0 copy-start.2
  3.0 1.2 %copy-done.2 = f32[2,320,384]{2,1,0:T(8,128)S(1)} copy-done((f32[2,320,384]{2,1,0:T(8,128)S(1)}, f32[2,320,384]{2,1,0:T(8,128)}, u32[]{:S(2)}) %copy-start.2) | copy-done | bytes 983064
  4.2 0.0 copy-start.3
  4.2 0.7 %copy-done.3 = f32[2,33]{1,0:T(2,128)S(1)} copy-done((f32[2,33]{1,0:T(2,128)S(1)}, f32[2,33]{1,0:T(2,128)}, u32[]{:S(2)}) %copy-start.3) | copy-done | bytes 288
  4.9 25.6 %shard_map.59 = (f32[2,320,384]{2,1,0:T(8,128)S(1)}, f32[2,320,384]{2,1,0:T(8,128)S(1)}) custom-call(f32[2,320,384]{2,1,0:T(8,128)S(1)} %copy-done, f32[2,320,384]{2,1,0:T(8,128)S(1)} %copy-done.1, f32[2,320,384]{2,1,0:T(8,128)S(1)} %copy-done.2, f32[2,33]{1,0:T(2,128)S(1)} %copy-done.3), custom_call_target="tpu_custom_call" | custom-call | flops 10000000000 | bytes 5000000 | tf_op jit(solution)/shard_map/pallas_call | solution.py:398
  30.6 0.9 %copy.8 = f32[2,320,384]{2,1,0:T(8,128)} copy(f32[2,320,384]{2,1,0:T(8,128)S(1)} %get-tuple-element.4) | data formatting | bytes 1966080
  31.5 0.9 %copy.9 = f32[2,320,384]{2,1,0:T(8,128)} copy(f32[2,320,384]{2,1,0:T(8,128)S(1)} %get-tuple-element.5) | data formatting | bytes 1966080
Async XLA Ops:
  0.6 1.2 %copy-start = (f32[2,320,384]{2,1,0:T(8,128)S(1)}, f32[2,320,384]{2,1,0:T(8,128)}, u32[]{:S(2)}) copy-start(f32[2,320,384]{2,1,0:T(8,128)} %inc.1) | copy-start | bytes 2949124
  1.8 1.2 %copy-start.1 = (f32[2,320,384]{2,1,0:T(8,128)S(1)}, f32[2,320,384]{2,1,0:T(8,128)}, u32[]{:S(2)}) copy-start(f32[2,320,384]{2,1,0:T(8,128)} %ph.1) | copy-start | bytes 2949124
  3.0 1.2 %copy-start.2 = (f32[2,320,384]{2,1,0:T(8,128)S(1)}, f32[2,320,384]{2,1,0:T(8,128)}, u32[]{:S(2)}) copy-start(f32[2,320,384]{2,1,0:T(8,128)} %cot.1) | copy-start | bytes 2949124
  4.2 0.7 %copy-start.3 = (f32[2,33]{1,0:T(2,128)S(1)}, f32[2,33]{1,0:T(2,128)}, u32[]{:S(2)}) copy-start(f32[2,33]{1,0:T(2,128)} %prop.1) | copy-start | bytes 796
where the time goes:
time: 32.7 us; the launch traced here: 32.5 us
  Pallas kernels  25.6 us (78%)
  local copies, waits for them, and re-layouts  6.17 us (19%)
  between operations  0.65 us (2%)
    pallas_call x1, Pallas kernels, on_device(): make_kernel(H, W, propagator.shape)(incident, phases, cotangent, propagator)  25.6 us
    unnamed x10, local copies, waits for them, and re-layouts  6.17 us

commit v1 on v0

--- a/solution.py
+++ b/solution.py
@@ -44,6 +44,28 @@
     return pltpu.roll(wide, shift % width, 1, stride=1, stride_axis=0)
 
 
+def down_pass(src_h, src_l, dst_h, dst_l, band, rows, lo_lane, hi_lane):
+    starts = list(range(0, rows - OUT, OUT)) + [rows - OUT]
+    cols = slice(lo_lane, hi_lane)
+    for q0 in starts:
+        win = slice(q0, q0 + LANES)
+        hi = [src_h[0, win, cols], src_h[1, win, cols]]
+        lo = [src_l[0, win, cols], src_l[1, win, cols]]
+        operand = jnp.concatenate(hi + lo + hi, axis=0)
+        u = jnp.dot(band[...], operand, preferred_element_type=F32)
+        h, l = split(u)
+        for p in range(2):
+            dst_h[p, q0 : q0 + OUT, cols] = h[p * OUT : (p + 1) * OUT]
+            dst_l[p, q0 : q0 + OUT, cols] = l[p * OUT : (p + 1) * OUT]
+
+
+def across(src_h, src_l, band, rows, t, tiles):
+    a, b = [slice(n * LANES, (n + 1) * LANES) for n in (t % (tiles + 1), (t + 1) % (tiles + 1))]
+    hi = [src_h[0, rows, a], src_h[0, rows, b], src_h[1, rows, a], src_h[1, rows, b]]
+    lo = [src_l[0, rows, a], src_l[0, rows, b], src_l[1, rows, a], src_l[1, rows, b]]
+    return jnp.dot(jnp.concatenate(hi + lo + hi, axis=1), band[...], preferred_element_type=F32)
+
+
 PIECES = (("c0", WIDE, 0), ("c1", WIDE, 32), ("p1", RIM, 64), ("i0", RIM, 80), ("i1", RIM, 96), ("p0", RIM, 112))
 
 
@@ -53,11 +75,11 @@
     step = block(H, 80)
 
     def kernel(
-        inc, ph, cot, prop, pg, pb,
+        inc, ph, cot, prop, gh, gl, pgv, wz, c0, s0, rowa, colb,
         incv, phv, cotv, packl, packr, hl, hr, crow, irow, prow,
-        taps, line, xh, xl, zh, zl, gh, gl, uh, ul, vh, vl,
-        c1, s1, c0, s0, wz, gout, fout, rowf, rowa, colf, cola, colb, pgv, pbv,
-        load, store, send, recv,
+        taps, line, xh, xl, zh, zl, uh, ul, vh, vl,
+        c1, s1, gout, fout, rowf, colf, cola,
+        load, send, recv,
     ):
         ty, tx = lax.axis_index("ty"), lax.axis_index("tx")
         ny, nx = lax.axis_size("ty"), lax.axis_size("tx")
@@ -206,28 +228,9 @@
                 zh[p, q, 0:W] = hi
                 zl[p, q, 0:W] = lo
 
-        def down_pass(src_h, src_l, dst_h, dst_l, band, rows, lo_lane, hi_lane):
-            starts = list(range(0, rows - OUT, OUT)) + [rows - OUT]
-            cols = slice(lo_lane, hi_lane)
-            for q0 in starts:
-                win = slice(q0, q0 + LANES)
-                hi = [src_h[0, win, cols], src_h[1, win, cols]]
-                lo = [src_l[0, win, cols], src_l[1, win, cols]]
-                operand = jnp.concatenate(hi + lo + hi, axis=0)
-                u = jnp.dot(band[...], operand, preferred_element_type=F32)
-                h, l = split(u)
-                for p in range(2):
-                    dst_h[p, q0 : q0 + OUT, cols] = h[p * OUT : (p + 1) * OUT]
-                    dst_l[p, q0 : q0 + OUT, cols] = l[p * OUT : (p + 1) * OUT]
-
-        def across_pass(src_h, src_l, dst, band, rows, which, first=0):
+        def across_pass(src_h, src_l, dst, band, rows, which):
             for t in which:
-                m, n = (t + first) % (tiles + 1), (t + first + 1) % (tiles + 1)
-                a, b = slice(m * LANES, (m + 1) * LANES), slice(n * LANES, (n + 1) * LANES)
-                hi = [src_h[0, 0:rows, a], src_h[0, 0:rows, b], src_h[1, 0:rows, a], src_h[1, 0:rows, b]]
-                lo = [src_l[0, 0:rows, a], src_l[0, 0:rows, b], src_l[1, 0:rows, a], src_l[1, 0:rows, b]]
-                operand = jnp.concatenate(hi + lo + hi, axis=1)
-                dst[t, 0:rows, :] = jnp.dot(operand, band[...], preferred_element_type=F32)
+                dst[t, 0:rows, :] = across(src_h, src_l, band, slice(0, rows), t, tiles)
 
         down_pass(xh, xl, uh, ul, rowa, H + WIDE, 0, W)
         down_pass(zh, zl, vh, vl, rowf, H, 0, W)
@@ -328,34 +331,11 @@
                 c, s = c1[q, cols], s1[q, cols]
                 term = pltpu.roll(gi * (fr * c - fi * s) - gr * (fr * s + fi * c), RIM, 1)
                 if before is not None:
-                    pgv[1, r, cols] = jnp.where(first, before, term)
+                    pgv[r, cols] = jnp.where(first, before, term)
                 before = term
 
-        stores = [pltpu.make_async_copy(pgv.at[1], pg.at[1], store.at[0])]
-        stores[0].start()
-
-        down_pass(gh, gl, vh, vl, rowa, H, 0, full)
-        across_pass(vh, vl, fout, colb, H, range(tiles), -1)
-
-        @pl.loop(0, H // fstep)
-        def _(i):
-            r = pl.ds(pl.multiple_of(i * fstep, 16), fstep)
-            for t in range(tiles):
-                cols = slice(t * LANES, (t + 1) * LANES)
-                gr, gi = fout[t, r, 0:LANES], fout[t, r, LANES : 2 * LANES]
-                c, s = c0[r, cols], s0[r, cols]
-                pgv[0, r, cols] = gi * wz[0, r, cols] - gr * wz[1, r, cols]
-                pbv[0, r, cols] = gr * c + gi * s
-                pbv[1, r, cols] = gi * c - gr * s
-
-        stores.append(pltpu.make_async_copy(pgv.at[0], pg.at[0], store.at[1]))
-        stores.append(pltpu.make_async_copy(pbv, pb, store.at[2]))
-        stores[1].start()
-        stores[2].start()
         for c in copies:
             c.wait_send()
-        for c in stores:
-            c.wait()
 
     V = pltpu.VMEM
     scratch = [
@@ -367,24 +347,24 @@
         V((2, H + 2 * WIDE, full), BF16), V((2, H + 2 * WIDE, full), BF16),
         V((2, H + WIDE, full), BF16), V((2, H + WIDE, full), BF16),
         V((2, H + WIDE, full), BF16), V((2, H + WIDE, full), BF16),
-        V((2, H + WIDE, full), BF16), V((2, H + WIDE, full), BF16),
         V((2, H, full), BF16), V((2, H, full), BF16),
         V((H + WIDE, full), F32), V((H + WIDE, full), F32),
-        V((H, W), F32), V((H, W), F32), V((2, H, W), F32),
         V((tiles + 1, H + WIDE, 2 * LANES), F32), V((tiles + 1, H, 2 * LANES), F32),
-        V((2 * OUT, 6 * LANES), BF16), V((2 * OUT, 6 * LANES), BF16),
+        V((2 * OUT, 6 * LANES), BF16),
         V((12 * LANES, 2 * LANES), BF16), V((12 * LANES, 2 * LANES), BF16),
-        V((12 * LANES, 2 * LANES), BF16),
-        V((2, H, W), F32), V((2, H, W), F32),
-        pltpu.SemaphoreType.DMA((4,)), pltpu.SemaphoreType.DMA((3,)),
+        pltpu.SemaphoreType.DMA((4,)),
         pltpu.SemaphoreType.DMA((12,)), pltpu.SemaphoreType.DMA((12,)),
     ]
-    anywhere = pl.BlockSpec(memory_space=pl.ANY)
+    results = (
+        V((2, H + WIDE, full), BF16), V((2, H + WIDE, full), BF16),
+        V((H, W), F32), V((2, H, W), F32), V((H, W), F32), V((H, W), F32),
+        V((2 * OUT, 6 * LANES), BF16), V((12 * LANES, 2 * LANES), BF16),
+    )
     return pl.pallas_call(
         kernel,
-        out_shape=(jax.ShapeDtypeStruct((2, H, W), F32), jax.ShapeDtypeStruct((2, H, W), F32)),
+        out_shape=results,
         in_specs=[pl.BlockSpec(memory_space=pltpu.HBM)] * 4,
-        out_specs=(anywhere, anywhere),
+        out_specs=tuple(pl.BlockSpec(memory_space=V) for _ in results),
         scratch_shapes=scratch,
         compiler_params=pltpu.CompilerParams(
             collective_id=0, has_side_effects=True, vmem_limit_bytes=40 * 1024 * 1024
@@ -393,9 +373,55 @@
     )
 
 
+def make_last(H, W):
+    tiles = W // LANES
+    step = block(H, 160)
+
+    def kernel(gh, gl, pgv, wz, c0, s0, rowa, colb, pg, pb, vh, vl, term, probe, store):
+        copies = []
+
+        def put(src, dst):
+            c = pltpu.make_async_copy(src, dst, store.at[len(copies)])
+            c.start()
+            copies.append(c)
+
+        put(pgv, pg.at[1])
+        down_pass(gh, gl, vh, vl, rowa, H, 0, W + LANES)
+        for r0 in range(0, H, step):
+            r = slice(r0, r0 + step)
+            for t in range(tiles):
+                cols = slice(t * LANES, (t + 1) * LANES)
+                g = across(vh, vl, colb, r, t - 1, tiles)
+                gr, gi = g[:, 0:LANES], g[:, LANES : 2 * LANES]
+                c, s = c0[r, cols], s0[r, cols]
+                term[r, cols] = gi * wz[0, r, cols] - gr * wz[1, r, cols]
+                probe[0, r, cols] = gr * c + gi * s
+                probe[1, r, cols] = gi * c - gr * s
+            put(term.at[r], pg.at[0, r])
+            put(probe.at[:, r], pb.at[:, r])
+        for c in copies:
+            c.wait()
+
+    V = pltpu.VMEM
+    out = jax.ShapeDtypeStruct((2, H, W), F32)
+    return pl.pallas_call(
+        kernel,
+        out_shape=(out, out),
+        in_specs=[pl.BlockSpec(memory_space=V)] * 8,
+        out_specs=(pl.BlockSpec(memory_space=pltpu.HBM),) * 2,
+        scratch_shapes=[
+            V((2, H, W + LANES), BF16), V((2, H, W + LANES), BF16), V((H, W), F32), V((2, H, W), F32),
+            pltpu.SemaphoreType.DMA((1 + 2 * (H // step),)),
+        ],
+        compiler_params=pltpu.CompilerParams(vmem_limit_bytes=32 * 1024 * 1024),
+        cost_estimate=pl.CostEstimate(flops=10**10, bytes_accessed=5 * 10**6, transcendentals=0),
+    )
+
+
 def on_device(incident, phases, cotangent, propagator):
     H, W = incident.shape[1], incident.shape[2]
-    return make_kernel(H, W, propagator.shape)(incident, phases, cotangent, propagator)
+    operands = [pltpu.with_memory_space_constraint(x, pltpu.HBM) for x in (incident, phases, cotangent, propagator)]
+    return make_last(H, W)(*make_kernel(H, W, propagator.shape)(*operands))
 
 
 def solution(mesh):

time: 32.7 us -> 24.6 us (0.75)
  local copies, waits for them, and re-layouts: 6.17 us -> 0 us
  Pallas kernels: 25.6 us -> 23.8 us
    unnamed x10 -> x0, local copies, waits for them, and re-layouts: 6.17 us -> none
    pallas_call x1 -> x2, Pallas kernels: 25.6 us -> 23.8 us  [on_device(): return make_last(H, W)(*make_kernel(H, W, propagator.shape)(*operands))]
where the time goes in v1:
time: 24.6 us; the launch traced here: 24.4 us
  Pallas kernels  23.8 us (97%)
  between operations  0.64 us (3%)
    pallas_call x2, Pallas kernels, on_device(): return make_last(H, W)(*make_kernel(H, W, propagator.shape)(*operands))  23.8 us

profile of v1, /device:TPU:1, one launch (start us, length us, event | category | flops | bytes accessed | tf_op | source)
XLA Modules:
  0.0 24.4 jit_solution(14674397465296768089)
XLA Ops:
  0.6 21.3 %shard_map.59 = (bf16[2,352,512]{2,1,0:T(8,128)(2,1)S(1)}, bf16[2,352,512]{2,1,0:T(8,128)(2,1)S(1)}, f32[320,384]{1,0:T(8,128)S(1)}, f32[2,320,384]{2,1,0:T(8,12...) custom-call(f32[2,320,384]{2,1,0:T(8,128)} %inc.1, ...), custom_call_target="tpu_custom_call" | custom-call | flops 10000000000 | bytes 5000000 | tf_op jit(solution)/shard_map/pallas_call | solution.py:424
  21.9 2.5 %shard_map.60 = (f32[2,320,384]{2,1,0:T(8,128)}, f32[2,320,384]{2,1,0:T(8,128)}) custom-call(bf16[2,352,512]{2,1,0:T(8,128)(2,1)S(1)} %get-tuple-element.10.gh, bf16[2,352,512]{2,1,0:T(8,128)(2,1)S(1)} %get-tuple-element.11.gl, f32[320,384]{1,0:T(8,128)S(1)} %get-tuple-element.12.pgv, f32[2,320,384]{2,1,0:T(8,128)S(1)} %get-tuple-element.13.wz, ...), custom_call_target="tpu_custom_call" | custom-call | flops 10000000000 | bytes 5000000 | tf_op jit(solution)/shard_map/pallas_call | solution.py:424

commit v2 on v1

--- a/solution.py
+++ b/solution.py
@@ -66,17 +66,31 @@
     return jnp.dot(jnp.concatenate(hi + lo + hi, axis=1), band[...], preferred_element_type=F32)
 
 
-PIECES = (("c0", WIDE, 0), ("c1", WIDE, 32), ("p1", RIM, 64), ("i0", RIM, 80), ("i1", RIM, 96), ("p0", RIM, 112))
+def weave(parts, rows):
+    lane = lanes_of(rows)
+    out = None
+    for value, src, dst in parts:
+        turn = (dst - src) % LANES
+        value = pltpu.roll(value, turn, 1) if turn else value
+        out = value if out is None else jnp.where(lane >= dst, value, out)
+    return out
+
+
+def edges(a, b, width, src):
+    lane = lanes_of(a.shape[0])
+    turn = (LANES - width - src) % LANES
+    a = pltpu.roll(a, turn, 1) if turn else a
+    b = pltpu.roll(b, -src % LANES, 1) if src else b
+    return jnp.where(lane < width, b, jnp.where(lane >= LANES - width, a, 0.0))
 
 
 def make_kernel(H, W, tap_shape):
     tiles = W // LANES
     full = W + LANES
-    step = block(H, 80)
 
     def kernel(
         inc, ph, cot, prop, gh, gl, pgv, wz, c0, s0, rowa, colb,
-        incv, phv, cotv, packl, packr, hl, hr, crow, irow, prow,
+        incv, phv, cotv, packl, packr, wavel, waver, corner, cl, cr, wl, wr, met, crow, irow, prow,
         taps, line, xh, xl, zh, zl, uh, ul, vh, vl,
         c1, s1, gout, fout, rowf, colf, cola,
         load, send, recv,
@@ -86,37 +100,30 @@
         up, down = lax.rem(ty + ny - 1, ny), lax.rem(ty + 1, ny)
         left, right = lax.rem(tx + nx - 1, nx), lax.rem(tx + 1, nx)
 
-        loads = [
-            pltpu.make_async_copy(src, dst, load.at[k])
-            for k, (src, dst) in enumerate(((cot, cotv), (ph, phv), (inc, incv), (prop, taps)))
-        ]
+        pairs = [(a.at[p], b.at[p]) for a, b, p in ((cot, cotv, 0), (cot, cotv, 1), (ph, phv, 1), (ph, phv, 0), (inc, incv, 0), (inc, incv, 1))]
+        loads = [pltpu.make_async_copy(src, dst, load.at[k]) for k, (src, dst) in enumerate(pairs + [(prop, taps)])]
         for c in loads:
             c.start()
         barrier = pltpu.get_barrier_semaphore()
         others = [(up, tx), (down, tx), (ty, left), (ty, right), (up, left), (up, right), (down, left), (down, right)]
         for dev in others:
             pl.semaphore_signal(barrier, inc=1, device_id=dev, device_id_type=pl.DeviceIdType.MESH)
-        for c in loads:
+
+        sides = ((slice(0, LANES), 0), (slice(W - LANES, W), 1))
+        part2, part4, part8 = H // 2, H // 4, H // 8
+        for c in loads[:3]:
             c.wait()
-
-        def plane(name):
-            return {"c0": (cotv, 0), "c1": (cotv, 1), "p0": (phv, 0), "p1": (phv, 1), "i0": (incv, 0), "i1": (incv, 1)}[name]
-
-        @pl.loop(0, H // step)
-        def _(i):
-            r = pl.ds(pl.multiple_of(i * step, step), step)
-            lane = lanes_of(step)
-            a = jnp.zeros((step, LANES), F32)
-            b = jnp.zeros((step, LANES), F32)
-            for name, w, dst in PIECES:
-                ref, p = plane(name)
-                first = ref[p, r, 0:LANES]
-                last = ref[p, r, W - LANES : W]
-                here = (lane >= dst) & (lane < dst + w)
-                a = jnp.where(here, pltpu.roll(first, dst, 1) if dst else first, a)
-                b = jnp.where(here, pltpu.roll(last, (dst + w) % LANES, 1), b)
-            packl[r, :] = a
-            packr[r, :] = b
+        for (cols, far), dst in zip(sides, (packl, packr)):
+            src = far * (LANES - WIDE)
+            for r0 in range(0, part2, part4):
+                dst[r0 : r0 + part4, :] = weave(
+                    [(cotv[p, g * part2 + r0 : g * part2 + r0 + part4, cols], src, 2 * WIDE * g + WIDE * p) for g in range(2) for p in range(2)],
+                    part4,
+                )
+            src = far * (LANES - RIM)
+            dst[part2 : part2 + part8, :] = weave(
+                [(phv[1, g * part8 : (g + 1) * part8, cols], src, RIM * g) for g in range(8)], part8
+            )
 
         pl.semaphore_wait(barrier, 8)
         copies = []
@@ -130,18 +137,52 @@
             c.start()
             copies.append(c)
 
-        push(packl, hr.at[WIDE : WIDE + H], (ty, left))
-        push(packr, hl.at[WIDE : WIDE + H], (ty, right))
+        push(packl, cr, (ty, left))
+        push(packr, cl, (ty, right))
         push(cot.at[:, 0:WIDE, :], crow.at[1], (up, tx))
         push(cot.at[:, H - WIDE : H, :], crow.at[0], (down, tx))
         push(inc.at[:, 0:RIM, :], irow.at[1], (up, tx))
         push(inc.at[:, H - RIM : H, :], irow.at[0], (down, tx))
         push(ph.at[:, 0:RIM, :], prow.at[1], (up, tx))
         push(ph.at[:, H - RIM : H, :], prow.at[0], (down, tx))
-        push(packl.at[0:WIDE], hr.at[WIDE + H : WIDE + H + WIDE], (up, left))
-        push(packl.at[H - WIDE : H], hr.at[0:WIDE], (down, left))
-        push(packr.at[0:WIDE], hl.at[WIDE + H : WIDE + H + WIDE], (up, right))
-        push(packr.at[H - WIDE : H], hl.at[0:WIDE], (down, right))
+
+        for c in loads[3:]:
+            c.wait()
+
+        @pl.loop(0, H // 16)
+        def _(i):
+            r0 = pl.multiple_of(i * 16, 16)
+            r = pl.ds(r0, 16)
+            q = pl.ds(pl.multiple_of(r0 + RIM, 16), 16)
+            s, c = sincos(phv[0, r, :])
+            s0[r, :] = s
+            c0[r, :] = c
+            a, b = incv[0, r, :], incv[1, r, :]
+            for p, w in enumerate((a * c - b * s, a * s + b * c)):
+                wz[p, r, :] = w
+                hi, lo = split(w)
+                zh[p, q, 0:W] = hi
+                zl[p, q, 0:W] = lo
+
+        for n, (cols, far) in enumerate(sides):
+            wide, rim = far * (LANES - WIDE), far * (LANES - RIM)
+            for m, r in enumerate((slice(0, WIDE), slice(H - WIDE, H))):
+                corner[n, m] = weave(
+                    [(cotv[0, r, cols], wide, 0), (cotv[1, r, cols], wide, WIDE), (phv[1, r, cols], rim, 2 * WIDE)]
+                    + [(wz[p, r, cols], rim, 2 * WIDE + RIM * (p + 1)) for p in range(2)],
+                    WIDE,
+                )
+        for (cols, far), dst in zip(sides, (wavel, waver)):
+            src = far * (LANES - RIM)
+            dst[...] = weave(
+                [(wz[p, g * part4 : (g + 1) * part4, cols], src, WIDE * g + RIM * p) for g in range(4) for p in range(2)], part4
+            )
+        push(corner.at[0, 0], met.at[1, 1], (up, left))
+        push(corner.at[0, 1], met.at[1, 0], (down, left))
+        push(corner.at[1, 0], met.at[0, 1], (up, right))
+        push(corner.at[1, 1], met.at[0, 0], (down, right))
+        push(wavel, wr, (ty, left))
+        push(waver, wl, (ty, right))
 
         line[...] = jnp.zeros(line.shape, F32)
         line[0:2, 0 : prop.shape[1]] = taps[...]
@@ -201,15 +242,6 @@
                 xl[p, q, 0:W] = lo
             q = pl.ds(pl.multiple_of(r0 + RIM, 16), 16)
             phase_one(phv, r, q, 16, range(tiles - 1))
-            s, c = sincos(phv[0, r, :])
-            s0[r, :] = s
-            c0[r, :] = c
-            a, b = incv[0, r, :], incv[1, r, :]
-            for p, w in enumerate((a * c - b * s, a * s + b * c)):
-                wz[p, r, :] = w
-                hi, lo = split(w)
-                zh[p, q, 0:W] = hi
-                zl[p, q, 0:W] = lo
 
         for k in (2, 3, 4, 5, 6, 7):
             copies[k].wait_recv()
@@ -240,66 +272,39 @@
         for k in (0, 1, 8, 9, 10, 11):
             copies[k].wait_recv()
         edge = slice(W, full)
-
-        def piece(a, b, index, rows):
-            _, w, dst = PIECES[index]
-            lane = lanes_of(rows)
-            a = pltpu.roll(a, (LANES - w - dst) % LANES, 1)
-            b = pltpu.roll(b, (-dst) % LANES, 1) if dst else b
-            return jnp.where(lane < w, b, jnp.where(lane >= LANES - w, a, 0.0))
-
-        xstep = block(H + 2 * WIDE, 96)
-
-        @pl.loop(0, (H + 2 * WIDE) // xstep)
-        def _(i):
-            r = pl.ds(pl.multiple_of(i * xstep, 16), xstep)
-            a, b = hl[r, :], hr[r, :]
-            for p in range(2):
-                hi, lo = split(piece(a, b, p, xstep))
-                xh[p, r, edge] = hi
-                xl[p, r, edge] = lo
-
-        estep = block(H + WIDE, 64)
-
-        def phase_edge(r, q, own, own_r, rows):
-            a, b = hl[q, :], hr[q, :]
-            _, _, dst = PIECES[2]
+        for p in range(2):
+            for g in range(2):
+                for r0 in range(0, part2, part4):
+                    r = slice(r0, r0 + part4)
+                    q = slice(WIDE + g * part2 + r0, WIDE + g * part2 + r0 + part4)
+                    xh[p, q, edge], xl[p, q, edge] = split(edges(cl[r, :], cr[r, :], WIDE, 2 * WIDE * g + WIDE * p))
+            for m, q in enumerate((slice(0, WIDE), slice(WIDE + H, 2 * WIDE + H))):
+                xh[p, q, edge], xl[p, q, edge] = split(edges(met[0, m], met[1, m], WIDE, WIDE * p))
+
+        down_pass(xh, xl, uh, ul, rowa, H + WIDE, W, full)
+        across_pass(uh, ul, gout, cola, H + WIDE, range(tiles - 1, tiles + 1))
+
+        def phase_edge(q, a, b, src, own, own_r, rows):
             lane = lanes_of(rows)
             inner = moved(own, tiles - 1, own_r)
-            x = jnp.where(lane >= LANES - RIM, pltpu.roll(b, LANES - RIM - dst, 1), inner)
-            outer = jnp.where(lane >= LANES - WIDE, pltpu.roll(a, LANES - WIDE - dst, 1), 0.0)
+            x = jnp.where(lane >= LANES - RIM, pltpu.roll(b, (LANES - RIM - src) % LANES, 1), inner)
+            outer = jnp.where(lane >= LANES - WIDE, pltpu.roll(a, (LANES - WIDE - src) % LANES, 1), 0.0)
             y = jnp.where(lane >= LANES - RIM, moved(own, 0, own_r), outer)
             for t, v in ((tiles - 1, x), (tiles, y)):
                 s, c = sincos(v)
-                s1[r, t * LANES : (t + 1) * LANES] = s
-                c1[r, t * LANES : (t + 1) * LANES] = c
-
-        hstep = block(H, 64)
-
-        @pl.loop(0, H // hstep)
-        def _(i):
-            r = pl.ds(pl.multiple_of(i * hstep + RIM, 16), hstep)
-            q = pl.ds(pl.multiple_of(i * hstep + WIDE, 16), hstep)
-            phase_edge(r, q, phv, pl.ds(pl.multiple_of(i * hstep, 16), hstep), hstep)
-
-        for side in range(2):
-            e = side * (H + RIM)
-            phase_edge(slice(e, e + RIM), slice(e + RIM, e + WIDE), prow.at[side], slice(0, RIM), RIM)
-
-        @pl.loop(0, (H + WIDE) // estep)
-        def _(i):
-            r = pl.ds(pl.multiple_of(i * estep, 16), estep)
-            q = pl.ds(pl.multiple_of(i * estep + RIM, 16), estep)
-            a, b = hl[q, :], hr[q, :]
-            s, c = sincos(piece(a, b, 5, estep))
-            x, y = piece(a, b, 3, estep), piece(a, b, 4, estep)
-            for p, w in enumerate((x * c - y * s, x * s + y * c)):
-                hi, lo = split(w)
-                zh[p, r, edge] = hi
-                zl[p, r, edge] = lo
-
-        down_pass(xh, xl, uh, ul, rowa, H + WIDE, W, full)
-        across_pass(uh, ul, gout, cola, H + WIDE, range(tiles - 1, tiles + 1))
+                s1[q, t * LANES : (t + 1) * LANES] = s
+                c1[q, t * LANES : (t + 1) * LANES] = c
+
+        for g in range(8):
+            r = slice(part2, part2 + part8)
+            q = slice(RIM + g * part8, RIM + (g + 1) * part8)
+            phase_edge(q, cl[r, :], cr[r, :], RIM * g, phv, slice(g * part8, (g + 1) * part8), part8)
+        near = (slice(RIM, WIDE), slice(0, RIM))
+        rims = (slice(0, RIM), slice(RIM + H, WIDE + H))
+        for m in range(2):
+            phase_edge(rims[m], met[0, m, near[m]], met[1, m, near[m]], 2 * WIDE, prow.at[m], slice(0, RIM), RIM)
+
+        estep = block(H + WIDE, 64)
 
         @pl.loop(0, (H + WIDE) // estep)
         def _(i):
@@ -312,6 +317,16 @@
                     hi, lo = split(g)
                     gh[p, r, cols] = hi
                     gl[p, r, cols] = lo
+
+        for k in (12, 13):
+            copies[k].wait_recv()
+        for p in range(2):
+            for g in range(4):
+                q = slice(RIM + g * part4, RIM + (g + 1) * part4)
+                zh[p, q, edge], zl[p, q, edge] = split(edges(wl[...], wr[...], RIM, WIDE * g + RIM * p))
+            for m in range(2):
+                value = edges(met[0, m, near[m]], met[1, m, near[m]], RIM, 2 * WIDE + RIM * (p + 1))
+                zh[p, rims[m], edge], zl[p, rims[m], edge] = split(value)
 
         down_pass(zh, zl, vh, vl, rowf, H, W, full)
         across_pass(vh, vl, fout, colf, H, range(tiles - 1, tiles + 1))
@@ -340,8 +355,10 @@
     V = pltpu.VMEM
     scratch = [
         V((2, H, W), F32), V((2, H, W), F32), V((2, H, W), F32),
-        V((H, LANES), F32), V((H, LANES), F32),
-        V((H + 2 * WIDE, LANES), F32), V((H + 2 * WIDE, LANES), F32),
+        V((H // 2 + H // 8, LANES), F32), V((H // 2 + H // 8, LANES), F32),
+        V((H // 4, LANES), F32), V((H // 4, LANES), F32), V((2, 2, WIDE, LANES), F32),
+        V((H // 2 + H // 8, LANES), F32), V((H // 2 + H // 8, LANES), F32),
+        V((H // 4, LANES), F32), V((H // 4, LANES), F32), V((2, 2, WIDE, LANES), F32),
         V((2, 2, WIDE, W), F32), V((2, 2, RIM, W), F32), V((2, 2, RIM, W), F32),
         V(tap_shape, F32), V((8, 2 * LANES), F32),
         V((2, H + 2 * WIDE, full), BF16), V((2, H + 2 * WIDE, full), BF16),
@@ -352,8 +369,8 @@
         V((tiles + 1, H + WIDE, 2 * LANES), F32), V((tiles + 1, H, 2 * LANES), F32),
         V((2 * OUT, 6 * LANES), BF16),
         V((12 * LANES, 2 * LANES), BF16), V((12 * LANES, 2 * LANES), BF16),
-        pltpu.SemaphoreType.DMA((4,)),
-        pltpu.SemaphoreType.DMA((12,)), pltpu.SemaphoreType.DMA((12,)),
+        pltpu.SemaphoreType.DMA((7,)),
+        pltpu.SemaphoreType.DMA((14,)), pltpu.SemaphoreType.DMA((14,)),
     ]
     results = (
         V((2, H + WIDE, full), BF16), V((2, H + WIDE, full), BF16),

time: 24.6 us -> 23.1 us (0.939)
  Pallas kernels: 23.8 us -> 22.4 us
    pallas_call x2, Pallas kernels: 23.8 us -> 22.4 us  [on_device(): return make_last(H, W)(*make_kernel(H, W, propagator.shape)(*operands))]
where the time goes in v2:
time: 23.1 us; the launch traced here: 23 us
  Pallas kernels  22.4 us (97%)
  between operations  0.64 us (3%)
    pallas_call x2, Pallas kernels, on_device(): return make_last(H, W)(*make_kernel(H, W, propagator.shape)(*operands))  22.4 us

profile of v2, /device:TPU:1, one launch (start us, length us, event | category | flops | bytes accessed | tf_op | source)
XLA Modules:
  0.0 23.0 jit_solution(5485936957903058253)
XLA Ops:
  0.6 19.8 %shard_map.59 = (bf16[2,352,512]{2,1,0:T(8,128)(2,1)S(1)}, bf16[2,352,512]{2,1,0:T(8,128)(2,1)S(1)}, f32[320,384]{1,0:T(8,128)S(1)}, f32[2,320,384]{2,1,0:T(8,12...) custom-call(f32[2,320,384]{2,1,0:T(8,128)} %inc.1, ...), custom_call_target="tpu_custom_call" | custom-call | flops 10000000000 | bytes 5000000 | tf_op jit(solution)/shard_map/pallas_call | solution.py:441
  20.5 2.5 %shard_map.60 = (f32[2,320,384]{2,1,0:T(8,128)}, f32[2,320,384]{2,1,0:T(8,128)}) custom-call(bf16[2,352,512]{2,1,0:T(8,128)(2,1)S(1)} %get-tuple-element.10.gh, bf16[2,352,512]{2,1,0:T(8,128)(2,1)S(1)} %get-tuple-element.11.gl, f32[320,384]{1,0:T(8,128)S(1)} %get-tuple-element.12.pgv, f32[2,320,384]{2,1,0:T(8,128)S(1)} %get-tuple-element.13.wz, ...), custom_call_target="tpu_custom_call" | custom-call | flops 10000000000 | bytes 5000000 | tf_op jit(solution)/shard_map/pallas_call | solution.py:441

commit v3 on v2

--- a/solution.py
+++ b/solution.py
@@ -44,8 +44,11 @@
     return pltpu.roll(wide, shift % width, 1, stride=1, stride_axis=0)
 
 
-def down_pass(src_h, src_l, dst_h, dst_l, band, rows, lo_lane, hi_lane):
-    starts = list(range(0, rows - OUT, OUT)) + [rows - OUT]
+def row_blocks(rows):
+    return list(range(0, rows - OUT, OUT)) + [rows - OUT]
+
+
+def down_pass(src_h, src_l, dst_h, dst_l, band, starts, lo_lane, hi_lane):
     cols = slice(lo_lane, hi_lane)
     for q0 in starts:
         win = slice(q0, q0 + LANES)
@@ -89,10 +92,10 @@
     full = W + LANES
 
     def kernel(
-        inc, ph, cot, prop, gh, gl, pgv, wz, c0, s0, rowa, colb,
-        incv, phv, cotv, packl, packr, wavel, waver, corner, cl, cr, wl, wr, met, crow, irow, prow,
-        taps, line, xh, xl, zh, zl, uh, ul, vh, vl,
-        c1, s1, gout, fout, rowf, colf, cola,
+        inc, ph, cot, prop, th, tl, pgv, wz, c0, s0, colb,
+        tilel, tiler, phasel, phaser, incv, phv, cotv, packl, packr, wavel, waver, corner, cl, cr, wl, wr, met, crow, irow, prow,
+        taps, line, xh, xl, zh, zl, gh, gl, uh, ul, vh, vl,
+        c1, s1, gout, fout, rowf, rowa, colf, cola,
         load, send, recv,
     ):
         ty, tx = lax.axis_index("ty"), lax.axis_index("tx")
@@ -100,6 +103,13 @@
         up, down = lax.rem(ty + ny - 1, ny), lax.rem(ty + 1, ny)
         left, right = lax.rem(tx + nx - 1, nx), lax.rem(tx + 1, nx)
 
+        near_edge = ((cot, slice(0, 2), tilel), (cot, slice(0, 2), tiler), (ph, 1, phasel), (ph, 1, phaser))
+        first = [
+            pltpu.make_async_copy(src.at[p, :, slice(0, LANES) if k % 2 == 0 else slice(W - LANES, W)], dst, load.at[7 + k])
+            for k, (src, p, dst) in enumerate(near_edge)
+        ]
+        for c in first:
+            c.start()
         pairs = [(a.at[p], b.at[p]) for a, b, p in ((cot, cotv, 0), (cot, cotv, 1), (ph, phv, 1), (ph, phv, 0), (inc, incv, 0), (inc, incv, 1))]
         loads = [pltpu.make_async_copy(src, dst, load.at[k]) for k, (src, dst) in enumerate(pairs + [(prop, taps)])]
         for c in loads:
@@ -111,34 +121,51 @@
 
         sides = ((slice(0, LANES), 0), (slice(W - LANES, W), 1))
         part2, part4, part8 = H // 2, H // 4, H // 8
-        for c in loads[:3]:
+        for c in first:
             c.wait()
-        for (cols, far), dst in zip(sides, (packl, packr)):
+        for far, cotx, phx, dst in ((0, tilel, phasel, packl), (1, tiler, phaser, packr)):
             src = far * (LANES - WIDE)
             for r0 in range(0, part2, part4):
                 dst[r0 : r0 + part4, :] = weave(
-                    [(cotv[p, g * part2 + r0 : g * part2 + r0 + part4, cols], src, 2 * WIDE * g + WIDE * p) for g in range(2) for p in range(2)],
+                    [(cotx[p, g * part2 + r0 : g * part2 + r0 + part4, :], src, 2 * WIDE * g + WIDE * p) for g in range(2) for p in range(2)],
                     part4,
                 )
             src = far * (LANES - RIM)
             dst[part2 : part2 + part8, :] = weave(
-                [(phv[1, g * part8 : (g + 1) * part8, cols], src, RIM * g) for g in range(8)], part8
+                [(phx[g * part8 : (g + 1) * part8, :], src, RIM * g) for g in range(8)], part8
             )
 
         pl.semaphore_wait(barrier, 8)
         copies = []
 
-        def push(src, dst, dev):
+        def push(src, dst, dev, start=True):
             k = len(copies)
             c = pltpu.make_async_remote_copy(
                 src_ref=src, dst_ref=dst, send_sem=send.at[k], recv_sem=recv.at[k],
                 device_id=dev, device_id_type=pl.DeviceIdType.MESH,
             )
-            c.start()
+            if start:
+                c.start()
             copies.append(c)
 
-        push(packl, cr, (ty, left))
-        push(packr, cl, (ty, right))
+        odd = lax.rem(tx, 2)
+
+        def push_both(to_left, to_right):
+            push(*to_left, (ty, left), start=False)
+            push(*to_right, (ty, right), start=False)
+            a, b = copies[-2:]
+
+            @pl.when(odd == 0)
+            def _():
+                a.start()
+                b.start()
+
+            @pl.when(odd == 1)
+            def _():
+                b.start()
+                a.start()
+
+        push_both((packl, cr), (packr, cl))
         push(cot.at[:, 0:WIDE, :], crow.at[1], (up, tx))
         push(cot.at[:, H - WIDE : H, :], crow.at[0], (down, tx))
         push(inc.at[:, 0:RIM, :], irow.at[1], (up, tx))
@@ -146,7 +173,7 @@
         push(ph.at[:, 0:RIM, :], prow.at[1], (up, tx))
         push(ph.at[:, H - RIM : H, :], prow.at[0], (down, tx))
 
-        for c in loads[3:]:
+        for c in loads:
             c.wait()
 
         @pl.loop(0, H // 16)
@@ -181,8 +208,7 @@
         push(corner.at[0, 1], met.at[1, 0], (down, left))
         push(corner.at[1, 0], met.at[0, 1], (up, right))
         push(corner.at[1, 1], met.at[0, 0], (down, right))
-        push(wavel, wr, (ty, left))
-        push(waver, wl, (ty, right))
+        push_both((wavel, wr), (waver, wl))
 
         line[...] = jnp.zeros(line.shape, F32)
         line[0:2, 0 : prop.shape[1]] = taps[...]
@@ -242,6 +268,12 @@
                 xl[p, q, 0:W] = lo
             q = pl.ds(pl.multiple_of(r0 + RIM, 16), 16)
             phase_one(phv, r, q, 16, range(tiles - 1))
+
+        xall, zall = row_blocks(H + WIDE), row_blocks(H)
+        xin = [q for q in xall if q >= WIDE and q + LANES <= WIDE + H]
+        zin = [q for q in zall if q >= RIM and q + LANES <= RIM + H]
+        down_pass(xh, xl, uh, ul, rowa, xin, 0, W)
+        down_pass(zh, zl, vh, vl, rowf, zin, 0, W)
 
         for k in (2, 3, 4, 5, 6, 7):
             copies[k].wait_recv()
@@ -264,10 +296,26 @@
             for t in which:
                 dst[t, 0:rows, :] = across(src_h, src_l, band, slice(0, rows), t, tiles)
 
-        down_pass(xh, xl, uh, ul, rowa, H + WIDE, 0, W)
-        down_pass(zh, zl, vh, vl, rowf, H, 0, W)
+        down_pass(xh, xl, uh, ul, rowa, [q for q in xall if q not in xin], 0, W)
+        down_pass(zh, zl, vh, vl, rowf, [q for q in zall if q not in zin], 0, W)
         across_pass(uh, ul, gout, cola, H + WIDE, range(tiles - 1))
         across_pass(vh, vl, fout, colf, H, range(tiles - 1))
+
+        estep = block(H + WIDE, 64)
+
+        def turn_back(which):
+            @pl.loop(0, (H + WIDE) // estep)
+            def _(i):
+                r = pl.ds(pl.multiple_of(i * estep, 16), estep)
+                for t in which:
+                    cols = slice(t * LANES, (t + 1) * LANES)
+                    gr, gi = gout[t, r, 0:LANES], gout[t, r, LANES : 2 * LANES]
+                    c, s = c1[r, cols], s1[r, cols]
+                    for p, g in enumerate((gr * c + gi * s, gi * c - gr * s)):
+                        gh[p, r, cols], gl[p, r, cols] = split(g)
+
+        turn_back(range(tiles - 1))
+        down_pass(gh, gl, th, tl, rowa, zall, 0, (tiles - 1) * LANES)
 
         for k in (0, 1, 8, 9, 10, 11):
             copies[k].wait_recv()
@@ -281,7 +329,7 @@
             for m, q in enumerate((slice(0, WIDE), slice(WIDE + H, 2 * WIDE + H))):
                 xh[p, q, edge], xl[p, q, edge] = split(edges(met[0, m], met[1, m], WIDE, WIDE * p))
 
-        down_pass(xh, xl, uh, ul, rowa, H + WIDE, W, full)
+        down_pass(xh, xl, uh, ul, rowa, xall, W, full)
         across_pass(uh, ul, gout, cola, H + WIDE, range(tiles - 1, tiles + 1))
 
         def phase_edge(q, a, b, src, own, own_r, rows):
@@ -304,19 +352,8 @@
         for m in range(2):
             phase_edge(rims[m], met[0, m, near[m]], met[1, m, near[m]], 2 * WIDE, prow.at[m], slice(0, RIM), RIM)
 
-        estep = block(H + WIDE, 64)
-
-        @pl.loop(0, (H + WIDE) // estep)
-        def _(i):
-            r = pl.ds(pl.multiple_of(i * estep, 16), estep)
-            for t in range(tiles + 1):
-                cols = slice(t * LANES, (t + 1) * LANES)
-                gr, gi = gout[t, r, 0:LANES], gout[t, r, LANES : 2 * LANES]
-                c, s = c1[r, cols], s1[r, cols]
-                for p, g in enumerate((gr * c + gi * s, gi * c - gr * s)):
-                    hi, lo = split(g)
-                    gh[p, r, cols] = hi
-                    gl[p, r, cols] = lo
+        turn_back(range(tiles - 1, tiles + 1))
+        down_pass(gh, gl, th, tl, rowa, zall, (tiles - 1) * LANES, full)
 
         for k in (12, 13):
             copies[k].wait_recv()
@@ -328,7 +365,7 @@
                 value = edges(met[0, m, near[m]], met[1, m, near[m]], RIM, 2 * WIDE + RIM * (p + 1))
                 zh[p, rims[m], edge], zl[p, rims[m], edge] = split(value)
 
-        down_pass(zh, zl, vh, vl, rowf, H, W, full)
+        down_pass(zh, zl, vh, vl, rowf, zall, W, full)
         across_pass(vh, vl, fout, colf, H, range(tiles - 1, tiles + 1))
 
         fstep = block(H, 32)
@@ -354,6 +391,7 @@
 
     V = pltpu.VMEM
     scratch = [
+        V((2, H, LANES), F32), V((2, H, LANES), F32), V((H, LANES), F32), V((H, LANES), F32),
         V((2, H, W), F32), V((2, H, W), F32), V((2, H, W), F32),
         V((H // 2 + H // 8, LANES), F32), V((H // 2 + H // 8, LANES), F32),
         V((H // 4, LANES), F32), V((H // 4, LANES), F32), V((2, 2, WIDE, LANES), F32),
@@ -364,18 +402,19 @@
         V((2, H + 2 * WIDE, full), BF16), V((2, H + 2 * WIDE, full), BF16),
         V((2, H + WIDE, full), BF16), V((2, H + WIDE, full), BF16),
         V((2, H + WIDE, full), BF16), V((2, H + WIDE, full), BF16),
+        V((2, H + WIDE, full), BF16), V((2, H + WIDE, full), BF16),
         V((2, H, full), BF16), V((2, H, full), BF16),
         V((H + WIDE, full), F32), V((H + WIDE, full), F32),
         V((tiles + 1, H + WIDE, 2 * LANES), F32), V((tiles + 1, H, 2 * LANES), F32),
-        V((2 * OUT, 6 * LANES), BF16),
+        V((2 * OUT, 6 * LANES), BF16), V((2 * OUT, 6 * LANES), BF16),
         V((12 * LANES, 2 * LANES), BF16), V((12 * LANES, 2 * LANES), BF16),
-        pltpu.SemaphoreType.DMA((7,)),
+        pltpu.SemaphoreType.DMA((11,)),
         pltpu.SemaphoreType.DMA((14,)), pltpu.SemaphoreType.DMA((14,)),
     ]
     results = (
-        V((2, H + WIDE, full), BF16), V((2, H + WIDE, full), BF16),
+        V((2, H, full), BF16), V((2, H, full), BF16),
         V((H, W), F32), V((2, H, W), F32), V((H, W), F32), V((H, W), F32),
-        V((2 * OUT, 6 * LANES), BF16), V((12 * LANES, 2 * LANES), BF16),
+        V((12 * LANES, 2 * LANES), BF16),
     )
     return pl.pallas_call(
         kernel,
@@ -394,7 +433,7 @@
     tiles = W // LANES
     step = block(H, 160)
 
-    def kernel(gh, gl, pgv, wz, c0, s0, rowa, colb, pg, pb, vh, vl, term, probe, store):
+    def kernel(th, tl, pgv, wz, c0, s0, colb, pg, pb, term, probe, store):
         copies = []
 
         def put(src, dst):
@@ -403,12 +442,11 @@
             copies.append(c)
 
         put(pgv, pg.at[1])
-        down_pass(gh, gl, vh, vl, rowa, H, 0, W + LANES)
         for r0 in range(0, H, step):
             r = slice(r0, r0 + step)
             for t in range(tiles):
                 cols = slice(t * LANES, (t + 1) * LANES)
-                g = across(vh, vl, colb, r, t - 1, tiles)
+                g = across(th, tl, colb, r, t - 1, tiles)
                 gr, gi = g[:, 0:LANES], g[:, LANES : 2 * LANES]
                 c, s = c0[r, cols], s0[r, cols]
                 term[r, cols] = gi * wz[0, r, cols] - gr * wz[1, r, cols]
@@ -424,10 +462,10 @@
     return pl.pallas_call(
         kernel,
         out_shape=(out, out),
-        in_specs=[pl.BlockSpec(memory_space=V)] * 8,
+        in_specs=[pl.BlockSpec(memory_space=V)] * 7,
         out_specs=(pl.BlockSpec(memory_space=pltpu.HBM),) * 2,
         scratch_shapes=[
-            V((2, H, W + LANES), BF16), V((2, H, W + LANES), BF16), V((H, W), F32), V((2, H, W), F32),
+            V((H, W), F32), V((2, H, W), F32),
             pltpu.SemaphoreType.DMA((1 + 2 * (H // step),)),
         ],
         compiler_params=pltpu.CompilerParams(vmem_limit_bytes=32 * 1024 * 1024),

time: 23.1 us -> 23 us (level)
  no operation moved by 1% of the time
where the time goes in v3:
time: 23 us; the launch traced here: 22.9 us
  Pallas kernels  22.2 us (97%)
  between operations  0.64 us (3%)
    pallas_call x2, Pallas kernels, on_device(): return make_last(H, W)(*make_kernel(H, W, propagator.shape)(*operands))  22.2 us

profile of v3, /device:TPU:1, one launch (start us, length us, event | category | flops | bytes accessed | tf_op | source)
XLA Modules:
  0.0 22.9 jit_solution(1483109950744488981)
XLA Ops:
  0.6 20.3 %shard_map.59 = (bf16[2,320,512]{2,1,0:T(8,128)(2,1)S(1)}, bf16[2,320,512]{2,1,0:T(8,128)(2,1)S(1)}, f32[320,384]{1,0:T(8,128)S(1)}, f32[2,320,384]{2,1,0:T(8,12...) custom-call(f32[2,320,384]{2,1,0:T(8,128)} %inc.1, f32[2,320,384]{2,1,0:T(8,128)} %ph.1, ...), custom_call_target="tpu_custom_call" | custom-call | flops 10000000000 | bytes 5000000 | tf_op jit(solution)/shard_map/pallas_call | solution.py:479
  21.0 1.9 %shard_map.60 = (f32[2,320,384]{2,1,0:T(8,128)}, f32[2,320,384]{2,1,0:T(8,128)}) custom-call(bf16[2,320,512]{2,1,0:T(8,128)(2,1)S(1)} %get-tuple-element.9.th, bf16[2,320,512]{2,1,0:T(8,128)(2,1)S(1)} %get-tuple-element.10.tl, f32[320,384]{1,0:T(8,128)S(1)} %get-tuple-element.11.pgv, f32[2,320,384]{2,1,0:T(8,128)S(1)} %get-tuple-element.12.wz, ...), custom_call_target="tpu_custom_call" | custom-call | flops 10000000000 | bytes 5000000 | tf_op jit(solution)/shard_map/pallas_call | solution.py:479

commit v4 on v3

--- a/solution.py
+++ b/solution.py
@@ -92,10 +92,10 @@
     full = W + LANES
 
     def kernel(
-        inc, ph, cot, prop, th, tl, pgv, wz, c0, s0, colb,
-        tilel, tiler, phasel, phaser, incv, phv, cotv, packl, packr, wavel, waver, corner, cl, cr, wl, wr, met, crow, irow, prow,
-        taps, line, xh, xl, zh, zl, gh, gl, uh, ul, vh, vl,
-        c1, s1, gout, fout, rowf, rowa, colf, cola,
+        inc, ph, cot, prop, gz, pgv, wz, c0, s0,
+        tilel, tiler, phasel, phaser, incv, phv, cotv, packl, packr, wavel, waver, cc, ww, metc, metp, metw, crow, irow, prow,
+        taps, line, xh, xl, zh, zl, gh, gl, uh, ul, vh, vl, th, tl,
+        c1, s1, gout, fout, rowf, rowa, colf, cola, colb,
         load, send, recv,
     ):
         ty, tx = lax.axis_index("ty"), lax.axis_index("tx")
@@ -115,7 +115,7 @@
         for c in loads:
             c.start()
         barrier = pltpu.get_barrier_semaphore()
-        others = [(up, tx), (down, tx), (ty, left), (ty, right), (up, left), (up, right), (down, left), (down, right)]
+        others = [(up, tx), (down, tx), (ty, left), (ty, right)]
         for dev in others:
             pl.semaphore_signal(barrier, inc=1, device_id=dev, device_id_type=pl.DeviceIdType.MESH)
 
@@ -135,7 +135,7 @@
                 [(phx[g * part8 : (g + 1) * part8, :], src, RIM * g) for g in range(8)], part8
             )
 
-        pl.semaphore_wait(barrier, 8)
+        pl.semaphore_wait(barrier, 4)
         copies = []
 
         def push(src, dst, dev, start=True):
@@ -165,7 +165,7 @@
                 b.start()
                 a.start()
 
-        push_both((packl, cr), (packr, cl))
+        push_both((packl, cc.at[1]), (packr, cc.at[0]))
         push(cot.at[:, 0:WIDE, :], crow.at[1], (up, tx))
         push(cot.at[:, H - WIDE : H, :], crow.at[0], (down, tx))
         push(inc.at[:, 0:RIM, :], irow.at[1], (up, tx))
@@ -191,24 +191,12 @@
                 zh[p, q, 0:W] = hi
                 zl[p, q, 0:W] = lo
 
-        for n, (cols, far) in enumerate(sides):
-            wide, rim = far * (LANES - WIDE), far * (LANES - RIM)
-            for m, r in enumerate((slice(0, WIDE), slice(H - WIDE, H))):
-                corner[n, m] = weave(
-                    [(cotv[0, r, cols], wide, 0), (cotv[1, r, cols], wide, WIDE), (phv[1, r, cols], rim, 2 * WIDE)]
-                    + [(wz[p, r, cols], rim, 2 * WIDE + RIM * (p + 1)) for p in range(2)],
-                    WIDE,
-                )
         for (cols, far), dst in zip(sides, (wavel, waver)):
             src = far * (LANES - RIM)
             dst[...] = weave(
                 [(wz[p, g * part4 : (g + 1) * part4, cols], src, WIDE * g + RIM * p) for g in range(4) for p in range(2)], part4
             )
-        push(corner.at[0, 0], met.at[1, 1], (up, left))
-        push(corner.at[0, 1], met.at[1, 0], (down, left))
-        push(corner.at[1, 0], met.at[0, 1], (up, right))
-        push(corner.at[1, 1], met.at[0, 0], (down, right))
-        push_both((wavel, wr), (waver, wl))
+        push_both((wavel, ww.at[1]), (waver, ww.at[0]))
 
         line[...] = jnp.zeros(line.shape, F32)
         line[0:2, 0 : prop.shape[1]] = taps[...]
@@ -275,8 +263,8 @@
         down_pass(xh, xl, uh, ul, rowa, xin, 0, W)
         down_pass(zh, zl, vh, vl, rowf, zin, 0, W)
 
-        for k in (2, 3, 4, 5, 6, 7):
-            copies[k].wait_recv()
+        for c in copies[2:8]:
+            c.wait_recv()
         for side in range(2):
             q = slice(0, WIDE) if side == 0 else slice(WIDE + H, WIDE + H + WIDE)
             for p in range(2):
@@ -317,20 +305,20 @@
         turn_back(range(tiles - 1))
         down_pass(gh, gl, th, tl, rowa, zall, 0, (tiles - 1) * LANES)
 
-        for k in (0, 1, 8, 9, 10, 11):
-            copies[k].wait_recv()
+        for c in copies[0:2]:
+            c.wait_recv()
+        push(cc.at[:, 0:WIDE], metc.at[1], (up, tx))
+        push(cc.at[:, part2 - WIDE : part2], metc.at[0], (down, tx))
+        push(cc.at[:, part2 : part2 + RIM], metp.at[1], (up, tx))
+        push(cc.at[:, part2 + part8 - RIM : part2 + part8], metp.at[0], (down, tx))
         edge = slice(W, full)
         for p in range(2):
             for g in range(2):
                 for r0 in range(0, part2, part4):
                     r = slice(r0, r0 + part4)
                     q = slice(WIDE + g * part2 + r0, WIDE + g * part2 + r0 + part4)
-                    xh[p, q, edge], xl[p, q, edge] = split(edges(cl[r, :], cr[r, :], WIDE, 2 * WIDE * g + WIDE * p))
-            for m, q in enumerate((slice(0, WIDE), slice(WIDE + H, 2 * WIDE + H))):
-                xh[p, q, edge], xl[p, q, edge] = split(edges(met[0, m], met[1, m], WIDE, WIDE * p))
-
-        down_pass(xh, xl, uh, ul, rowa, xall, W, full)
-        across_pass(uh, ul, gout, cola, H + WIDE, range(tiles - 1, tiles + 1))
+                    xh[p, q, edge], xl[p, q, edge] = split(edges(cc[0, r, :], cc[1, r, :], WIDE, 2 * WIDE * g + WIDE * p))
+        down_pass(xh, xl, uh, ul, rowa, xin, W, full)
 
         def phase_edge(q, a, b, src, own, own_r, rows):
             lane = lanes_of(rows)
@@ -346,26 +334,38 @@
         for g in range(8):
             r = slice(part2, part2 + part8)
             q = slice(RIM + g * part8, RIM + (g + 1) * part8)
-            phase_edge(q, cl[r, :], cr[r, :], RIM * g, phv, slice(g * part8, (g + 1) * part8), part8)
-        near = (slice(RIM, WIDE), slice(0, RIM))
+            phase_edge(q, cc[0, r, :], cc[1, r, :], RIM * g, phv, slice(g * part8, (g + 1) * part8), part8)
+        for c in copies[10:14]:
+            c.wait_recv()
         rims = (slice(0, RIM), slice(RIM + H, WIDE + H))
-        for m in range(2):
-            phase_edge(rims[m], met[0, m, near[m]], met[1, m, near[m]], 2 * WIDE, prow.at[m], slice(0, RIM), RIM)
+        for m, q in enumerate((slice(0, WIDE), slice(WIDE + H, 2 * WIDE + H))):
+            for p in range(2):
+                xh[p, q, edge], xl[p, q, edge] = split(edges(metc[m, 0], metc[m, 1], WIDE, (1 - m) * 2 * WIDE + WIDE * p))
+            phase_edge(rims[m], metp[m, 0], metp[m, 1], (1 - m) * 7 * RIM, prow.at[m], slice(0, RIM), RIM)
+        down_pass(xh, xl, uh, ul, rowa, [q for q in xall if q not in xin], W, full)
+        across_pass(uh, ul, gout, cola, H + WIDE, range(tiles - 1, tiles + 1))
 
         turn_back(range(tiles - 1, tiles + 1))
         down_pass(gh, gl, th, tl, rowa, zall, (tiles - 1) * LANES, full)
 
-        for k in (12, 13):
-            copies[k].wait_recv()
+        for c in copies[8:10]:
+            c.wait_recv()
+        push(ww.at[:, 0:RIM], metw.at[1], (up, tx))
+        push(ww.at[:, part4 - RIM : part4], metw.at[0], (down, tx))
         for p in range(2):
             for g in range(4):
                 q = slice(RIM + g * part4, RIM + (g + 1) * part4)
-                zh[p, q, edge], zl[p, q, edge] = split(edges(wl[...], wr[...], RIM, WIDE * g + RIM * p))
-            for m in range(2):
-                value = edges(met[0, m, near[m]], met[1, m, near[m]], RIM, 2 * WIDE + RIM * (p + 1))
+                zh[p, q, edge], zl[p, q, edge] = split(edges(ww[0], ww[1], RIM, WIDE * g + RIM * p))
+        down_pass(zh, zl, vh, vl, rowf, zin, W, full)
+        for t in range(tiles):
+            gz[t] = across(th, tl, colb, slice(0, H), t - 1, tiles)
+        for c in copies[14:16]:
+            c.wait_recv()
+        for m in range(2):
+            for p in range(2):
+                value = edges(metw[m, 0], metw[m, 1], RIM, (1 - m) * 3 * WIDE + RIM * p)
                 zh[p, rims[m], edge], zl[p, rims[m], edge] = split(value)
-
-        down_pass(zh, zl, vh, vl, rowf, zall, W, full)
+        down_pass(zh, zl, vh, vl, rowf, [q for q in zall if q not in zin], W, full)
         across_pass(vh, vl, fout, colf, H, range(tiles - 1, tiles + 1))
 
         fstep = block(H, 32)
@@ -394,9 +394,9 @@
         V((2, H, LANES), F32), V((2, H, LANES), F32), V((H, LANES), F32), V((H, LANES), F32),
         V((2, H, W), F32), V((2, H, W), F32), V((2, H, W), F32),
         V((H // 2 + H // 8, LANES), F32), V((H // 2 + H // 8, LANES), F32),
-        V((H // 4, LANES), F32), V((H // 4, LANES), F32), V((2, 2, WIDE, LANES), F32),
-        V((H // 2 + H // 8, LANES), F32), V((H // 2 + H // 8, LANES), F32),
-        V((H // 4, LANES), F32), V((H // 4, LANES), F32), V((2, 2, WIDE, LANES), F32),
+        V((H // 4, LANES), F32), V((H // 4, LANES), F32),
+        V((2, H // 2 + H // 8, LANES), F32), V((2, H // 4, LANES), F32),
+        V((2, 2, WIDE, LANES), F32), V((2, 2, RIM, LANES), F32), V((2, 2, RIM, LANES), F32),
         V((2, 2, WIDE, W), F32), V((2, 2, RIM, W), F32), V((2, 2, RIM, W), F32),
         V(tap_shape, F32), V((8, 2 * LANES), F32),
         V((2, H + 2 * WIDE, full), BF16), V((2, H + 2 * WIDE, full), BF16),
@@ -404,17 +404,17 @@
         V((2, H + WIDE, full), BF16), V((2, H + WIDE, full), BF16),
         V((2, H + WIDE, full), BF16), V((2, H + WIDE, full), BF16),
         V((2, H, full), BF16), V((2, H, full), BF16),
+        V((2, H, full), BF16), V((2, H, full), BF16),
         V((H + WIDE, full), F32), V((H + WIDE, full), F32),
         V((tiles + 1, H + WIDE, 2 * LANES), F32), V((tiles + 1, H, 2 * LANES), F32),
         V((2 * OUT, 6 * LANES), BF16), V((2 * OUT, 6 * LANES), BF16),
-        V((12 * LANES, 2 * LANES), BF16), V((12 * LANES, 2 * LANES), BF16),
+        V((12 * LANES, 2 * LANES), BF16), V((12 * LANES, 2 * LANES), BF16), V((12 * LANES, 2 * LANES), BF16),
         pltpu.SemaphoreType.DMA((11,)),
-        pltpu.SemaphoreType.DMA((14,)), pltpu.SemaphoreType.DMA((14,)),
+        pltpu.SemaphoreType.DMA((16,)), pltpu.SemaphoreType.DMA((16,)),
     ]
     results = (
-        V((2, H, full), BF16), V((2, H, full), BF16),
+        V((tiles, H, 2 * LANES), F32),
         V((H, W), F32), V((2, H, W), F32), V((H, W), F32), V((H, W), F32),
-        V((12 * LANES, 2 * LANES), BF16),
     )
     return pl.pallas_call(
         kernel,
@@ -431,9 +431,9 @@
 
 def make_last(H, W):
     tiles = W // LANES
-    step = block(H, 160)
-
-    def kernel(th, tl, pgv, wz, c0, s0, colb, pg, pb, term, probe, store):
+    step = block(H, 80)
+
+    def kernel(gz, pgv, wz, c0, s0, pg, pb, term, probe, store):
         copies = []
 
         def put(src, dst):
@@ -446,8 +446,7 @@
             r = slice(r0, r0 + step)
             for t in range(tiles):
                 cols = slice(t * LANES, (t + 1) * LANES)
-                g = across(th, tl, colb, r, t - 1, tiles)
-                gr, gi = g[:, 0:LANES], g[:, LANES : 2 * LANES]
+                gr, gi = gz[t, r, 0:LANES], gz[t, r, LANES : 2 * LANES]
                 c, s = c0[r, cols], s0[r, cols]
                 term[r, cols] = gi * wz[0, r, cols] - gr * wz[1, r, cols]
                 probe[0, r, cols] = gr * c + gi * s
@@ -462,14 +461,14 @@
     return pl.pallas_call(
         kernel,
         out_shape=(out, out),
-        in_specs=[pl.BlockSpec(memory_space=V)] * 7,
+        in_specs=[pl.BlockSpec(memory_space=V)] * 5,
         out_specs=(pl.BlockSpec(memory_space=pltpu.HBM),) * 2,
         scratch_shapes=[
             V((H, W), F32), V((2, H, W), F32),
             pltpu.SemaphoreType.DMA((1 + 2 * (H // step),)),
         ],
         compiler_params=pltpu.CompilerParams(vmem_limit_bytes=32 * 1024 * 1024),
-        cost_estimate=pl.CostEstimate(flops=10**10, bytes_accessed=5 * 10**6, transcendentals=0),
+        cost_estimate=pl.CostEstimate(flops=10**6, bytes_accessed=5 * 10**6, transcendentals=0),
     )
 
 

time: 23 us -> 25.9 us (1.13)
  Pallas kernels: 22.2 us -> 25.1 us
    pallas_call x2, Pallas kernels: 22.2 us -> 25.1 us  [on_device(): return make_last(H, W)(*make_kernel(H, W, propagator.shape)(*operands))]
where the time goes in v4:
time: 25.9 us; the launch traced here: 25.7 us
  Pallas kernels  25.1 us (97%)
  between operations  0.64 us (2%)
    pallas_call x2, Pallas kernels, on_device(): return make_last(H, W)(*make_kernel(H, W, propagator.shape)(*operands))  25.1 us

profile of v4, /device:TPU:1, one launch (start us, length us, event | category | flops | bytes accessed | tf_op | source)
XLA Modules:
  0.0 25.7 jit_solution(3104272615070467393)
XLA Ops:
  0.6 23.8 %shard_map.59 = (f32[3,320,256]{2,1,0:T(8,128)S(1)}, f32[320,384]{1,0:T(8,128)S(1)}, f32[2,320,384]{2,1,0:T(8,128)S(1)}, f32[320,384]{1,0:T(8,128)S(1)}, f32[320,384]{1,0:T(8,128)S(1)}) custom-call(f32[2,320,384]{2,1,0:T(8,128)} %inc.1, f32[2,320,384]{2,1,0:T(8,128)} %ph.1, f32[2,320,384]{2,1,0:T(8,128)} %cot.1, f32[2,33]{1,0:T(2,128)} %prop.1), custom_call_target="tpu_custom_call" | custom-call | flops 10000000000 | bytes 5000000 | tf_op jit(solution)/shard_map/pallas_call | solution.py:478
  24.4 1.3 %shard_map.60 = (f32[2,320,384]{2,1,0:T(8,128)}, f32[2,320,384]{2,1,0:T(8,128)}) custom-call(f32[3,320,256]{2,1,0:T(8,128)S(1)} %get-tuple-element.7.gz, f32[320,384]{1,0:T(8,128)S(1)} %get-tuple-element.8.pgv, f32[2,320,384]{2,1,0:T(8,128)S(1)} %get-tuple-element.9.wz, f32[320,384]{1,0:T(8,128)S(1)} %get-tuple-element.10.c0, ...), custom_call_target="tpu_custom_call" | custom-call | flops 1000000 | bytes 5000000 | tf_op jit(solution)/shard_map/pallas_call | solution.py:478

commit v5 on v3

--- a/solution.py
+++ b/solution.py
@@ -176,7 +176,7 @@
         for c in loads:
             c.wait()
 
-        @pl.loop(0, H // 16)
+        @pl.loop(0, H // 16, unroll=H // 16)
         def _(i):
             r0 = pl.multiple_of(i * 16, 16)
             r = pl.ds(r0, 16)
@@ -257,7 +257,7 @@
                 s1[q, t * LANES : (t + 1) * LANES] = s
                 c1[q, t * LANES : (t + 1) * LANES] = c
 
-        @pl.loop(0, H // 16)
+        @pl.loop(0, H // 16, unroll=H // 16)
         def _(i):
             r0 = pl.multiple_of(i * 16, 16)
             r = pl.ds(r0, 16)
@@ -304,7 +304,7 @@
         estep = block(H + WIDE, 64)
 
         def turn_back(which):
-            @pl.loop(0, (H + WIDE) // estep)
+            @pl.loop(0, (H + WIDE) // estep, unroll=(H + WIDE) // estep)
             def _(i):
                 r = pl.ds(pl.multiple_of(i * estep, 16), estep)
                 for t in which:
@@ -370,7 +370,7 @@
 
         fstep = block(H, 32)
 
-        @pl.loop(0, H // fstep)
+        @pl.loop(0, H // fstep, unroll=H // fstep)
         def _(i):
             r = pl.ds(pl.multiple_of(i * fstep, 16), fstep)
             q = pl.ds(pl.multiple_of(i * fstep + RIM, 16), fstep)

time: 23 us -> 21.6 us (0.939)
  Pallas kernels: 22.2 us -> 20.9 us
    pallas_call x2, Pallas kernels: 22.2 us -> 20.9 us  [on_device(): return make_last(H, W)(*make_kernel(H, W, propagator.shape)(*operands))]
where the time goes in v5:
time: 21.6 us; the launch traced here: 21.5 us
  Pallas kernels  20.9 us (97%)
  between operations  0.64 us (3%)
    pallas_call x2, Pallas kernels, on_device(): return make_last(H, W)(*make_kernel(H, W, propagator.shape)(*operands))  20.9 us

profile of v5, /device:TPU:1, one launch (start us, length us, event | category | flops | bytes accessed | tf_op | source)
XLA Modules:
  0.0 21.5 jit_solution(15599822732638086913)
XLA Ops:
  0.6 19.0 %shard_map.59 = (bf16[2,320,512]{2,1,0:T(8,128)(2,1)S(1)}, bf16[2,320,512]{2,1,0:T(8,128)(2,1)S(1)}, f32[320,384]{1,0:T(8,128)S(1)}, f32[2,320,384]{2,1,0:T(8,12...) custom-call(f32[2,320,384]{2,1,0:T(8,128)} %inc.1, f32[2,320,384]{2,1,0:T(8,128)} %ph.1, ...), custom_call_target="tpu_custom_call" | custom-call | flops 10000000000 | bytes 5000000 | tf_op jit(solution)/shard_map/pallas_call | solution.py:479
  19.6 1.9 %shard_map.60 = (f32[2,320,384]{2,1,0:T(8,128)}, f32[2,320,384]{2,1,0:T(8,128)}) custom-call(bf16[2,320,512]{2,1,0:T(8,128)(2,1)S(1)} %get-tuple-element.9.th, bf16[2,320,512]{2,1,0:T(8,128)(2,1)S(1)} %get-tuple-element.10.tl, f32[320,384]{1,0:T(8,128)S(1)} %get-tuple-element.11.pgv, f32[2,320,384]{2,1,0:T(8,128)S(1)} %get-tuple-element.12.wz, ...), custom_call_target="tpu_custom_call" | custom-call | flops 10000000000 | bytes 5000000 | tf_op jit(solution)/shard_map/pallas_call | solution.py:479

commit v6 on v5

--- a/solution.py
+++ b/solution.py
@@ -92,10 +92,10 @@
     full = W + LANES
 
     def kernel(
-        inc, ph, cot, prop, th, tl, pgv, wz, c0, s0, colb,
-        tilel, tiler, phasel, phaser, incv, phv, cotv, packl, packr, wavel, waver, corner, cl, cr, wl, wr, met, crow, irow, prow,
-        taps, line, xh, xl, zh, zl, gh, gl, uh, ul, vh, vl,
-        c1, s1, gout, fout, rowf, rowa, colf, cola,
+        inc, ph, cot, prop, gz, pgv, wz, c0, s0,
+        tilel, tiler, phasel, phaser, incv, phv, cotv, packl, packr, wavel, waver, cornc, corns, cl, cr, wl, wr, metc, mets, crow, irow, prow,
+        taps, line, xh, xl, zh, zl, gh, gl, uh, ul, vh, vl, th, tl,
+        c1, s1, gout, fout, rowf, rowa, colf, cola, colb,
         load, send, recv,
     ):
         ty, tx = lax.axis_index("ty"), lax.axis_index("tx")
@@ -135,6 +135,12 @@
                 [(phx[g * part8 : (g + 1) * part8, :], src, RIM * g) for g in range(8)], part8
             )
 
+            for m, r0 in enumerate((0, H - WIDE)):
+                cornc[far, m] = weave(
+                    [(cotx[p, r0 + RIM * g : r0 + RIM * (g + 1), :], far * (LANES - WIDE), 2 * WIDE * g + WIDE * p) for g in range(2) for p in range(2)],
+                    RIM,
+                )
+
         pl.semaphore_wait(barrier, 8)
         copies = []
 
@@ -165,6 +171,12 @@
                 b.start()
                 a.start()
 
+        def push_corners(src, dst):
+            push(src.at[0, 0], dst.at[1, 1], (up, left))
+            push(src.at[0, 1], dst.at[1, 0], (down, left))
+            push(src.at[1, 0], dst.at[0, 1], (up, right))
+            push(src.at[1, 1], dst.at[0, 0], (down, right))
+
         push_both((packl, cr), (packr, cl))
         push(cot.at[:, 0:WIDE, :], crow.at[1], (up, tx))
         push(cot.at[:, H - WIDE : H, :], crow.at[0], (down, tx))
@@ -172,6 +184,7 @@
         push(inc.at[:, H - RIM : H, :], irow.at[0], (down, tx))
         push(ph.at[:, 0:RIM, :], prow.at[1], (up, tx))
         push(ph.at[:, H - RIM : H, :], prow.at[0], (down, tx))
+        push_corners(cornc, metc)
 
         for c in loads:
             c.wait()
@@ -191,23 +204,21 @@
                 zh[p, q, 0:W] = hi
                 zl[p, q, 0:W] = lo
 
-        for n, (cols, far) in enumerate(sides):
-            wide, rim = far * (LANES - WIDE), far * (LANES - RIM)
-            for m, r in enumerate((slice(0, WIDE), slice(H - WIDE, H))):
-                corner[n, m] = weave(
-                    [(cotv[0, r, cols], wide, 0), (cotv[1, r, cols], wide, WIDE), (phv[1, r, cols], rim, 2 * WIDE)]
-                    + [(wz[p, r, cols], rim, 2 * WIDE + RIM * (p + 1)) for p in range(2)],
-                    WIDE,
+        for cols, far in sides:
+            rim = far * (LANES - RIM)
+            for m, r0 in enumerate((0, H - RIM)):
+                halves = [slice(r0 + 8 * g, r0 + 8 * (g + 1)) for g in range(2)]
+                corns[far, m] = weave(
+                    [(phv[1, r, cols], rim, RIM * g) for g, r in enumerate(halves)]
+                    + [(wz[p, r, cols], rim, WIDE + WIDE * g + RIM * p) for g, r in enumerate(halves) for p in range(2)],
+                    8,
                 )
         for (cols, far), dst in zip(sides, (wavel, waver)):
             src = far * (LANES - RIM)
             dst[...] = weave(
                 [(wz[p, g * part4 : (g + 1) * part4, cols], src, WIDE * g + RIM * p) for g in range(4) for p in range(2)], part4
             )
-        push(corner.at[0, 0], met.at[1, 1], (up, left))
-        push(corner.at[0, 1], met.at[1, 0], (down, left))
-        push(corner.at[1, 0], met.at[0, 1], (up, right))
-        push(corner.at[1, 1], met.at[0, 0], (down, right))
+        push_corners(corns, mets)
         push_both((wavel, wr), (waver, wl))
 
         line[...] = jnp.zeros(line.shape, F32)
@@ -326,8 +337,10 @@
                     r = slice(r0, r0 + part4)
                     q = slice(WIDE + g * part2 + r0, WIDE + g * part2 + r0 + part4)
                     xh[p, q, edge], xl[p, q, edge] = split(edges(cl[r, :], cr[r, :], WIDE, 2 * WIDE * g + WIDE * p))
-            for m, q in enumerate((slice(0, WIDE), slice(WIDE + H, 2 * WIDE + H))):
-                xh[p, q, edge], xl[p, q, edge] = split(edges(met[0, m], met[1, m], WIDE, WIDE * p))
+            for m, e in enumerate((0, WIDE + H)):
+                for g in range(2):
+                    q = slice(e + RIM * g, e + RIM * (g + 1))
+                    xh[p, q, edge], xl[p, q, edge] = split(edges(metc[0, m], metc[1, m], WIDE, 2 * WIDE * g + WIDE * p))
 
         down_pass(xh, xl, uh, ul, rowa, xall, W, full)
         across_pass(uh, ul, gout, cola, H + WIDE, range(tiles - 1, tiles + 1))
@@ -347,23 +360,28 @@
             r = slice(part2, part2 + part8)
             q = slice(RIM + g * part8, RIM + (g + 1) * part8)
             phase_edge(q, cl[r, :], cr[r, :], RIM * g, phv, slice(g * part8, (g + 1) * part8), part8)
-        near = (slice(RIM, WIDE), slice(0, RIM))
+        for c in copies[12:16]:
+            c.wait_recv()
         rims = (slice(0, RIM), slice(RIM + H, WIDE + H))
         for m in range(2):
-            phase_edge(rims[m], met[0, m, near[m]], met[1, m, near[m]], 2 * WIDE, prow.at[m], slice(0, RIM), RIM)
-
+            for g in range(2):
+                q = slice(rims[m].start + 8 * g, rims[m].start + 8 * (g + 1))
+                phase_edge(q, mets[0, m], mets[1, m], RIM * g, prow.at[m], slice(8 * g, 8 * (g + 1)), 8)
         turn_back(range(tiles - 1, tiles + 1))
         down_pass(gh, gl, th, tl, rowa, zall, (tiles - 1) * LANES, full)
 
-        for k in (12, 13):
-            copies[k].wait_recv()
+        for t in range(tiles):
+            gz[t] = across(th, tl, colb, slice(0, H), t - 1, tiles)
+
+        for c in copies[16:18]:
+            c.wait_recv()
         for p in range(2):
             for g in range(4):
                 q = slice(RIM + g * part4, RIM + (g + 1) * part4)
                 zh[p, q, edge], zl[p, q, edge] = split(edges(wl[...], wr[...], RIM, WIDE * g + RIM * p))
             for m in range(2):
-                value = edges(met[0, m, near[m]], met[1, m, near[m]], RIM, 2 * WIDE + RIM * (p + 1))
-                zh[p, rims[m], edge], zl[p, rims[m], edge] = split(value)
+                value = [edges(mets[0, m], mets[1, m], RIM, WIDE + WIDE * g + RIM * p) for g in range(2)]
+                zh[p, rims[m], edge], zl[p, rims[m], edge] = split(jnp.concatenate(value, axis=0))
 
         down_pass(zh, zl, vh, vl, rowf, zall, W, full)
         across_pass(vh, vl, fout, colf, H, range(tiles - 1, tiles + 1))
@@ -394,9 +412,9 @@
         V((2, H, LANES), F32), V((2, H, LANES), F32), V((H, LANES), F32), V((H, LANES), F32),
         V((2, H, W), F32), V((2, H, W), F32), V((2, H, W), F32),
         V((H // 2 + H // 8, LANES), F32), V((H // 2 + H // 8, LANES), F32),
-        V((H // 4, LANES), F32), V((H // 4, LANES), F32), V((2, 2, WIDE, LANES), F32),
+        V((H // 4, LANES), F32), V((H // 4, LANES), F32), V((2, 2, RIM, LANES), F32), V((2, 2, 8, LANES), F32),
         V((H // 2 + H // 8, LANES), F32), V((H // 2 + H // 8, LANES), F32),
-        V((H // 4, LANES), F32), V((H // 4, LANES), F32), V((2, 2, WIDE, LANES), F32),
+        V((H // 4, LANES), F32), V((H // 4, LANES), F32), V((2, 2, RIM, LANES), F32), V((2, 2, 8, LANES), F32),
         V((2, 2, WIDE, W), F32), V((2, 2, RIM, W), F32), V((2, 2, RIM, W), F32),
         V(tap_shape, F32), V((8, 2 * LANES), F32),
         V((2, H + 2 * WIDE, full), BF16), V((2, H + 2 * WIDE, full), BF16),
@@ -404,17 +422,17 @@
         V((2, H + WIDE, full), BF16), V((2, H + WIDE, full), BF16),
         V((2, H + WIDE, full), BF16), V((2, H + WIDE, full), BF16),
         V((2, H, full), BF16), V((2, H, full), BF16),
+        V((2, H, full), BF16), V((2, H, full), BF16),
         V((H + WIDE, full), F32), V((H + WIDE, full), F32),
         V((tiles + 1, H + WIDE, 2 * LANES), F32), V((tiles + 1, H, 2 * LANES), F32),
         V((2 * OUT, 6 * LANES), BF16), V((2 * OUT, 6 * LANES), BF16),
-        V((12 * LANES, 2 * LANES), BF16), V((12 * LANES, 2 * LANES), BF16),
+        V((12 * LANES, 2 * LANES), BF16), V((12 * LANES, 2 * LANES), BF16), V((12 * LANES, 2 * LANES), BF16),
         pltpu.SemaphoreType.DMA((11,)),
-        pltpu.SemaphoreType.DMA((14,)), pltpu.SemaphoreType.DMA((14,)),
+        pltpu.SemaphoreType.DMA((18,)), pltpu.SemaphoreType.DMA((18,)),
     ]
     results = (
-        V((2, H, full), BF16), V((2, H, full), BF16),
+        V((tiles, H, 2 * LANES), F32),
         V((H, W), F32), V((2, H, W), F32), V((H, W), F32), V((H, W), F32),
-        V((12 * LANES, 2 * LANES), BF16),
     )
     return pl.pallas_call(
         kernel,
@@ -431,9 +449,9 @@
 
 def make_last(H, W):
     tiles = W // LANES
-    step = block(H, 160)
-
-    def kernel(th, tl, pgv, wz, c0, s0, colb, pg, pb, term, probe, store):
+    step = block(H, 80)
+
+    def kernel(gz, pgv, wz, c0, s0, pg, pb, term, probe, store):
         copies = []
 
         def put(src, dst):
@@ -446,8 +464,7 @@
             r = slice(r0, r0 + step)
             for t in range(tiles):
                 cols = slice(t * LANES, (t + 1) * LANES)
-                g = across(th, tl, colb, r, t - 1, tiles)
-                gr, gi = g[:, 0:LANES], g[:, LANES : 2 * LANES]
+                gr, gi = gz[t, r, 0:LANES], gz[t, r, LANES : 2 * LANES]
                 c, s = c0[r, cols], s0[r, cols]
                 term[r, cols] = gi * wz[0, r, cols] - gr * wz[1, r, cols]
                 probe[0, r, cols] = gr * c + gi * s
@@ -462,7 +479,7 @@
     return pl.pallas_call(
         kernel,
         out_shape=(out, out),
-        in_specs=[pl.BlockSpec(memory_space=V)] * 7,
+        in_specs=[pl.BlockSpec(memory_space=V)] * 5,
         out_specs=(pl.BlockSpec(memory_space=pltpu.HBM),) * 2,
         scratch_shapes=[
             V((H, W), F32), V((2, H, W), F32),

time: 21.6 us -> 22.3 us (1.032)
  Pallas kernels: 20.9 us -> 21.5 us
    pallas_call x2, Pallas kernels: 20.9 us -> 21.5 us  [on_device(): return make_last(H, W)(*make_kernel(H, W, propagator.shape)(*operands))]
where the time goes in v6:
time: 22.3 us; the launch traced here: 22.1 us
  Pallas kernels  21.5 us (96%)
  between operations  0.64 us (3%)
    pallas_call x2, Pallas kernels, on_device(): return make_last(H, W)(*make_kernel(H, W, propagator.shape)(*operands))  21.5 us

profile of v6, /device:TPU:1, one launch (start us, length us, event | category | flops | bytes accessed | tf_op | source)
XLA Modules:
  0.0 22.1 jit_solution(5803901520485889769)
XLA Ops:
  0.6 20.2 %shard_map.59 = (f32[3,320,256]{2,1,0:T(8,128)S(1)}, f32[320,384]{1,0:T(8,128)S(1)}, f32[2,320,384]{2,1,0:T(8,128)S(1)}, f32[320,384]{1,0:T(8,128)S(1)}, f32[320,384]{1,0:T(8,128)S(1)}) custom-call(f32[2,320,384]{2,1,0:T(8,128)} %inc.1, f32[2,320,384]{2,1,0:T(8,128)} %ph.1, f32[2,320,384]{2,1,0:T(8,128)} %cot.1, f32[2,33]{1,0:T(2,128)} %prop.1), custom_call_target="tpu_custom_call" | custom-call | flops 10000000000 | bytes 5000000 | tf_op jit(solution)/shard_map/pallas_call | solution.py:496
  20.8 1.3 %shard_map.60 = (f32[2,320,384]{2,1,0:T(8,128)}, f32[2,320,384]{2,1,0:T(8,128)}) custom-call(f32[3,320,256]{2,1,0:T(8,128)S(1)} %get-tuple-element.7.gz, f32[320,384]{1,0:T(8,128)S(1)} %get-tuple-element.8.pgv, f32[2,320,384]{2,1,0:T(8,128)S(1)} %get-tuple-element.9.wz, f32[320,384]{1,0:T(8,128)S(1)} %get-tuple-element.10.c0, ...), custom_call_target="tpu_custom_call" | custom-call | flops 10000000000 | bytes 5000000 | tf_op jit(solution)/shard_map/pallas_call | solution.py:496

commit v7 on v5

--- a/solution.py
+++ b/solution.py
@@ -119,6 +119,43 @@
         for dev in others:
             pl.semaphore_signal(barrier, inc=1, device_id=dev, device_id_type=pl.DeviceIdType.MESH)
 
+        pl.semaphore_wait(barrier, 8)
+        copies = []
+
+        def push(src, dst, dev, start=True):
+            k = len(copies)
+            c = pltpu.make_async_remote_copy(
+                src_ref=src, dst_ref=dst, send_sem=send.at[k], recv_sem=recv.at[k],
+                device_id=dev, device_id_type=pl.DeviceIdType.MESH,
+            )
+            if start:
+                c.start()
+            copies.append(c)
+
+        odd = lax.rem(tx, 2)
+
+        def push_both(to_left, to_right):
+            push(*to_left, (ty, left), start=False)
+            push(*to_right, (ty, right), start=False)
+            a, b = copies[-2:]
+
+            @pl.when(odd == 0)
+            def _():
+                a.start()
+                b.start()
+
+            @pl.when(odd == 1)
+            def _():
+                b.start()
+                a.start()
+
+        push(cot.at[:, 0:WIDE, :], crow.at[1], (up, tx))
+        push(cot.at[:, H - WIDE : H, :], crow.at[0], (down, tx))
+        push(inc.at[:, 0:RIM, :], irow.at[1], (up, tx))
+        push(inc.at[:, H - RIM : H, :], irow.at[0], (down, tx))
+        push(ph.at[:, 0:RIM, :], prow.at[1], (up, tx))
+        push(ph.at[:, H - RIM : H, :], prow.at[0], (down, tx))
+
         sides = ((slice(0, LANES), 0), (slice(W - LANES, W), 1))
         part2, part4, part8 = H // 2, H // 4, H // 8
         for c in first:
@@ -134,44 +171,7 @@
             dst[part2 : part2 + part8, :] = weave(
                 [(phx[g * part8 : (g + 1) * part8, :], src, RIM * g) for g in range(8)], part8
             )
-
-        pl.semaphore_wait(barrier, 8)
-        copies = []
-
-        def push(src, dst, dev, start=True):
-            k = len(copies)
-            c = pltpu.make_async_remote_copy(
-                src_ref=src, dst_ref=dst, send_sem=send.at[k], recv_sem=recv.at[k],
-                device_id=dev, device_id_type=pl.DeviceIdType.MESH,
-            )
-            if start:
-                c.start()
-            copies.append(c)
-
-        odd = lax.rem(tx, 2)
-
-        def push_both(to_left, to_right):
-            push(*to_left, (ty, left), start=False)
-            push(*to_right, (ty, right), start=False)
-            a, b = copies[-2:]
-
-            @pl.when(odd == 0)
-            def _():
-                a.start()
-                b.start()
-
-            @pl.when(odd == 1)
-            def _():
-                b.start()
-                a.start()
-
         push_both((packl, cr), (packr, cl))
-        push(cot.at[:, 0:WIDE, :], crow.at[1], (up, tx))
-        push(cot.at[:, H - WIDE : H, :], crow.at[0], (down, tx))
-        push(inc.at[:, 0:RIM, :], irow.at[1], (up, tx))
-        push(inc.at[:, H - RIM : H, :], irow.at[0], (down, tx))
-        push(ph.at[:, 0:RIM, :], prow.at[1], (up, tx))
-        push(ph.at[:, H - RIM : H, :], prow.at[0], (down, tx))
 
         for c in loads:
             c.wait()
@@ -275,7 +275,7 @@
         down_pass(xh, xl, uh, ul, rowa, xin, 0, W)
         down_pass(zh, zl, vh, vl, rowf, zin, 0, W)
 
-        for k in (2, 3, 4, 5, 6, 7):
+        for k in (0, 1, 2, 3, 4, 5):
             copies[k].wait_recv()
         for side in range(2):
             q = slice(0, WIDE) if side == 0 else slice(WIDE + H, WIDE + H + WIDE)
@@ -317,7 +317,7 @@
         turn_back(range(tiles - 1))
         down_pass(gh, gl, th, tl, rowa, zall, 0, (tiles - 1) * LANES)
 
-        for k in (0, 1, 8, 9, 10, 11):
+        for k in (6, 7, 8, 9, 10, 11):
             copies[k].wait_recv()
         edge = slice(W, full)
         for p in range(2):

time: 21.6 us -> 21.7 us (level)
  no operation moved by 1% of the time
where the time goes in v7:
time: 21.7 us; the launch traced here: 21.6 us
  Pallas kernels  21 us (97%)
  between operations  0.64 us (3%)
    pallas_call x2, Pallas kernels, on_device(): return make_last(H, W)(*make_kernel(H, W, propagator.shape)(*operands))  21 us

profile of v7, /device:TPU:1, one launch (start us, length us, event | category | flops | bytes accessed | tf_op | source)
XLA Modules:
  0.0 21.6 jit_solution(6109803241265558794)
XLA Ops:
  0.6 19.1 %shard_map.59 = (bf16[2,320,512]{2,1,0:T(8,128)(2,1)S(1)}, bf16[2,320,512]{2,1,0:T(8,128)(2,1)S(1)}, f32[320,384]{1,0:T(8,128)S(1)}, f32[2,320,384]{2,1,0:T(8,12...) custom-call(f32[2,320,384]{2,1,0:T(8,128)} %inc.1, f32[2,320,384]{2,1,0:T(8,128)} %ph.1, ...), custom_call_target="tpu_custom_call" | custom-call | flops 10000000000 | bytes 5000000 | tf_op jit(solution)/shard_map/pallas_call | solution.py:479
  19.7 1.9 %shard_map.60 = (f32[2,320,384]{2,1,0:T(8,128)}, f32[2,320,384]{2,1,0:T(8,128)}) custom-call(bf16[2,320,512]{2,1,0:T(8,128)(2,1)S(1)} %get-tuple-element.9.th, bf16[2,320,512]{2,1,0:T(8,128)(2,1)S(1)} %get-tuple-element.10.tl, f32[320,384]{1,0:T(8,128)S(1)} %get-tuple-element.11.pgv, f32[2,320,384]{2,1,0:T(8,128)S(1)} %get-tuple-element.12.wz, ...), custom_call_target="tpu_custom_call" | custom-call | flops 10000000000 | bytes 5000000 | tf_op jit(solution)/shard_map/pallas_call | solution.py:479
